TPU v7x, 32 devices: a whole 2x2x4 slice. The times are simulated.
32 devices in a mesh: seq: 8 (over y, x, core), batch: 4 (over z).
Axes of the slice: x: 2, y: 2, z: 4, core: 2. Of those that a mesh axis runs over, the one named last changes fastest.
Arguments:
- inputs: bfloat16 [32, 8192, 512], P('batch', 'seq'), may hold values from -32 to 32
- ln_gain: float32 [512], P(('seq', 'batch')), may hold values from 0.1 to 1.9
- ln_bias: float32 [512], P(('seq', 'batch')), may hold values from -3 to 3
- w_in: bfloat16 [512, 1024], P(('seq', 'batch')), may hold values from -0.25 to 0.25
- b_in: float32 [1024], P(('seq', 'batch')), may hold values from -3 to 3
- w_depth: float32 [512, 31], P(('seq', 'batch')), may hold values from -1 to 1
- bn_gain: float32 [512], P(('seq', 'batch')), may hold values from 0.1 to 1.9
- bn_bias: float32 [512], P(('seq', 'batch')), may hold values from -3 to 3
- w_out: bfloat16 [512, 512], P(('seq', 'batch')), may hold values from -0.25 to 0.25
- b_out: float32 [512], P(('seq', 'batch')), may hold values from -3 to 3
Outputs:
- result: float32 [32, 8192, 512], P('batch', 'seq')
All inputs are finite; a program needn't handle non-finite values.
Results may differ from a plain program's by a relative error of at most 0.0015.
Values may be sent and summed in bfloat16 or wider, within the bound.
No kernel may reach another device: no remote copies, remote signals or barrier semaphores. Data moves between devices by JAX's collectives and lax.ppermute only.
A program may use at most 192 MiB of HBM per device.

v0:
```python
import jax
import jax.numpy as jnp
from jax import lax
from jax.sharding import PartitionSpec as P

EPSILON = 1e-05


def extended_2(cells, sides, width):
    for axis, dim in sides:
        count = lax.axis_size(axis)
        ends = count - 1
        head = lax.slice_in_dim(cells, 0, width, axis=dim)
        tail = lax.slice_in_dim(cells, cells.shape[dim] - width, cells.shape[dim], axis=dim)
        cells = jnp.concatenate(
            [
                lax.ppermute(tail, axis, [(i, (i + 1) % count) for i in range(ends)]),
                cells,
                lax.ppermute(head, axis, [((i + 1) % count, i) for i in range(ends)]),
            ],
            axis=dim,
        )
    return cells


def layer_normed(rows, ln_gain, ln_bias):
    centre = jnp.mean(rows, axis=-1, keepdims=True)
    spread = jnp.mean((rows - centre) ** 2, axis=-1, keepdims=True)
    return ((rows - centre) * lax.rsqrt(spread + EPSILON) * ln_gain + ln_bias).astype(jnp.bfloat16)


def fold_rows(left_rows, piece):
    return jnp.dot(left_rows, piece, preferred_element_type=jnp.float32)


def shards(inputs, ln_gain, ln_bias, w_in, b_in, w_depth, bn_gain, bn_bias, w_out, b_out):
    ln_gain, ln_bias, b_in, w_depth, bn_gain, bn_bias, b_out = (
        lax.all_gather(ln_gain, ("seq", "batch"), axis=0, tiled=True),
        lax.all_gather(ln_bias, ("seq", "batch"), axis=0, tiled=True),
        lax.all_gather(b_in, ("seq", "batch"), axis=0, tiled=True),
        lax.all_gather(w_depth, ("seq", "batch"), axis=0, tiled=True),
        lax.all_gather(bn_gain, ("seq", "batch"), axis=0, tiled=True),
        lax.all_gather(bn_bias, ("seq", "batch"), axis=0, tiled=True),
        lax.all_gather(b_out, ("seq", "batch"), axis=0, tiled=True),
    )
    seq_count, frame_count, width = inputs.shape
    half_width = (w_depth.shape[1] - 1) // 2
    normed = layer_normed(inputs.astype(jnp.float32), ln_gain, ln_bias)
    extended = extended_2(normed, (("seq", 1),), half_width)
    ext_frames = extended.shape[1]
    flat_rows = extended.reshape(seq_count * ext_frames, width)
    hidden = fold_rows(flat_rows, lax.all_gather(w_in, ("seq", "batch"), axis=0, tiled=True))
    hidden = hidden + b_in
    glu = (hidden[:, :width] * jax.nn.sigmoid(hidden[:, width:])).reshape(
        seq_count, ext_frames, width
    )
    position = lax.broadcasted_iota(jnp.int32, (1, ext_frames, 1), 1)
    seq_index = lax.axis_index("seq")
    keep_left = (position >= half_width) | (seq_index > 0)
    keep_right = (position < frame_count + half_width) | (seq_index < lax.axis_size("seq") - 1)
    padded = jnp.where(keep_left & keep_right, glu, 0.0)
    conv_out = jnp.zeros((seq_count, frame_count, width), jnp.float32)
    for tap_index in range(w_depth.shape[1]):
        conv_out = (
            conv_out + padded[:, tap_index : tap_index + frame_count, :] * w_depth[:, tap_index]
        )
    count = float(seq_count * frame_count * lax.axis_size("seq") * lax.axis_size("batch"))
    channel_total = lax.psum(jnp.sum(conv_out, axis=(0, 1)), ("seq", "batch"))
    mean_value = channel_total / count
    deviation_sum = lax.psum(jnp.sum((conv_out - mean_value) ** 2, axis=(0, 1)), ("seq", "batch"))
    variance = deviation_sum / count
    scale_factor = bn_gain * lax.rsqrt(variance + EPSILON)
    normal_act = (conv_out - mean_value) * scale_factor + bn_bias
    act_rows = (
        (normal_act * jax.nn.sigmoid(normal_act))
        .astype(jnp.bfloat16)
        .reshape(seq_count * frame_count, width)
    )
    projected = fold_rows(act_rows, lax.all_gather(w_out, ("seq", "batch"), axis=0, tiled=True))
    combined = (
        projected + b_out + inputs.reshape(seq_count * frame_count, width).astype(jnp.float32)
    )
    return combined.reshape(seq_count, frame_count, width)


def solution(mesh):
    return jax.shard_map(
        shards,
        mesh=mesh,
        in_specs=(
            P("batch", "seq", None),
            P(("seq", "batch")),
            P(("seq", "batch")),
            P(("seq", "batch"), None),
            P(("seq", "batch")),
            P(("seq", "batch"), None),
            P(("seq", "batch")),
            P(("seq", "batch")),
            P(("seq", "batch"), None),
            P(("seq", "batch")),
        ),
        out_specs=P("batch", "seq", None),
        check_vma=False,
    )
```

profile of v0, /device:TPU:0, one launch (start us, length us, event | category | flops | bytes accessed | tf_op | source)
XLA Modules:
  0.0 512.5 jit_solution(2028273680014701016)
XLA Ops:
  7.3 4.6 convert_reduce_fusion
  11.9 5.8 %multiply_reduce_fusion.1 = f32[8,1024]{1,0:T(8,128)S(1)} fusion(bf16[8,1024,512]{2,1,0:T(8,128)(2,1)} %param.10, f32[8,1024]{1,0:T(8,128)S(1)} %broadcast_multiply_fusion), kind=kLoop, calls=%fused_computation.71 | loop fusion | flops 16769024 | bytes 8454144 | tf_op jit(solution)/shard_map/reduce_sum | solution.py:28
  18.5 42.1 %all-reduce.7 = (f32[512]{0:T(512)S(1)}, f32[512]{0:T(512)S(1)}, f32[1024]{0:T(1024)S(1)}) all-reduce(f32[512]{0:T(512)S(1)} %dynamic-update-slice.1, f32[512]{0:T(512)S(1)} %dynamic-update-slice, f32[1024]{0:T(1024)S(1)} %dynamic-update-slice.2), channel_id=1, replica_groups=mesh['seq'=8,'batch'=4] {'seq','batch'}, use_global_device_ids=true, to_apply=%add.1 | all-reduce | flops 2048 | bytes 16384
  60.6 5.9 %add_convert_fusion = bf16[8,1024,512]{2,1,0:T(8,128)(2,1)S(1)} fusion(bf16[8,1024,512]{2,1,0:T(8,128)(2,1)} %param.10, f32[512]{0:T(512)S(1)} %get-tuple-element.40, f32[512]{0:T(512)S(1)} %get-tuple-element.41, f32[8,1024]{1,0:T(8,128)S(1)} %add_rsqrt_fusion, f32[8,1024]{1,0:T(8,128)S(1)} %broadcast_multiply_fusion), kind=kLoop, calls=%fused_computation.70 | loop fusion | flops 25165824 | bytes 16846848 | tf_op jit(solution)/shard_map/convert_element_type | solution.py:29
  66.6 1.7 collective-permute-start
  68.3 1.4 copy-done
  69.7 1.3 collective-permute-start.1
  71.0 70.2 %all_gather.31 = f32[512,31]{1,0:T(8,128)S(1)} all-gather(f32[16,31]{1,0:T(8,128)S(1)} %copy-done.3), channel_id=1, replica_groups=mesh['seq'=8,'batch'=4] {'seq','batch'}, dimensions={0}, use_global_device_ids=true | all-gather | bytes 65472 | tf_op jit(solution)/shard_map/all_gather | solution.py:41
  141.2 2.6 slice_reduce_fusion.30
  143.9 73.1 %all_gather.34 = bf16[512,512]{1,0:T(8,128)(2,1)} all-gather(bf16[16,512]{1,0:T(8,128)(2,1)S(1)} %copy-done.2), channel_id=1, replica_groups=mesh['seq'=8,'batch'=4] {'seq','batch'}, dimensions={0}, use_global_device_ids=true | all-gather | bytes 540672 | tf_op jit(solution)/shard_map/all_gather | solution.py:79
  216.9 1.7 slice_reduce_fusion.29
  220.0 1.4 dynamic-update-slice.5
  221.4 43.7 %concatenate.3 = bf16[8,1054,512]{2,1,0:T(8,128)(2,1)} concatenate(bf16[8,15,512]{2,1,0:T(8,128)(2,1)S(1)} %collective-permute-done, bf16[8,1024,512]{2,1,0:T(8,128)(2,1)} %copy-done, bf16[8,15,512]{2,1,0:T(8,128)(2,1)S(1)} %collective-permute-done.1), dimensions={1} | concatenate | bytes 17268736 | tf_op jit(solution)/shard_map/concatenate | solution.py:15
  265.1 10.8 %reshape.80 = bf16[8432,512]{1,0:T(8,128)(2,1)} reshape(bf16[8,1054,512]{2,1,0:T(8,128)(2,1)} %concatenate.3) | data formatting | bytes 17268736 | tf_op jit(solution)/shard_map/reshape | solution.py:51
  275.9 18.3 %convolution_add_fusion = f32[8432,1024]{1,0:T(8,128)} fusion(bf16[8432,512]{1,0:T(8,128)(2,1)} %reshape.80, bf16[512,1024]{1,0:T(8,128)(2,1)} %all-gather.2.cloned.1.call-done, f32[1024]{0:T(1024)S(1)} %get-tuple-element.42), kind=kOutput, calls=%fused_computation | convolution fusion | flops 8850227200 | bytes 44224512 | tf_op jit(solution)/shard_map/dot_general | solution.py:33
  294.1 18.4 %fusion.3 = f32[8432,512]{1,0:T(8,128)} fusion(f32[8432,1024]{1,0:T(8,128)} %convolution_add_fusion), kind=kLoop, calls=%fused_computation.5 | loop fusion | flops 17268736 | bytes 51806208 | tf_op jit(solution)/shard_map/mul | solution.py:54
  312.5 15.4 %reshape.81 = f32[8,1054,512]{2,1,0:T(8,128)} reshape(f32[8432,512]{1,0:T(8,128)} %fusion.3) | data formatting | bytes 34537472 | tf_op jit(solution)/shard_map/reshape | solution.py:54
  328.0 7.4 %broadcast_select_fusion = f32[8,1054,512]{2,1,0:T(8,128)S(1)} fusion(f32[8,1054,512]{2,1,0:T(8,128)} %reshape.81, pred[1054]{0:T(1024)(128)(4,1)S(1)} %fusion.35), kind=kLoop, calls=%fused_computation.73 | loop fusion | flops 4317184 | bytes 34538528 | tf_op jit(solution)/shard_map/jit(_where)/select_n | solution.py:61
  335.3 64.7 %fusion.37 = (f32[512]{0:T(512)S(1)}, f32[8,1024,512]{2,1,0:T(8,128)}) fusion(f32[512]{0:T(512)S(1)} %get-tuple-element.6, f32[8,1054,512]{2,1,0:T(8,128)S(1)} %broadcast_select_fusion, f32[512]{0:T(512)S(1)} %get-tuple-element.7, f32[512]{0:T(512)S(1)} %get-tuple-element.8, f32[512]{0:T(512)S(1)} %get-tuple-element.9, f32[512]{0:T(512)S(1)} %get-tuple-element.10, ...), kind=kLoop, calls=%fused_computation.114 | loop fusion | flops 260046336 | bytes 536936448 | tf_op jit(solution)/shard_map/reduce_sum | solution.py:68
  400.0 39.4 %psum.14 = f32[512]{0:T(512)S(1)} all-reduce(f32[512]{0:T(512)S(1)} %get-tuple-element.43), channel_id=1, replica_groups=mesh['seq'=8,'batch'=4] {'seq','batch'}, use_global_device_ids=true, to_apply=%region_3.4 | all-reduce | flops 512 | bytes 4096 | tf_op jit(solution)/shard_map/psum | solution.py:68
  439.5 7.6 %multiply_reduce_fusion = f32[512]{0:T(512)S(1)} fusion(f32[8,1024,512]{2,1,0:T(8,128)} %get-tuple-element.44, f32[512]{0:T(512)S(1)} %broadcast_multiply_fusion.1), kind=kLoop, calls=%fused_computation.69 | loop fusion | flops 12582400 | bytes 16781312 | tf_op jit(solution)/shard_map/reduce_sum | solution.py:70
  447.1 40.3 %all-reduce.6 = (f32[512]{0:T(512)S(1)}, f32[512]{0:T(512)S(1)}, f32[512]{0:T(512)S(1)}, f32[512]{0:T(512)S(1)}) all-reduce(f32[512]{0:T(512)S(1)} %copy-done.7, f32[512]{0:T(512)S(1)} %copy-done.5, f32[512]{0:T(512)S(1)} %multiply_reduce_fusion, f32[512]{0:T(512)} %dynamic-update-slice.5), channel_id=1, replica_groups=mesh['seq'=8,'batch'=4] {'seq','batch'}, use_global_device_ids=true, to_apply=%add.4 | all-reduce | flops 2048 | bytes 16384
  487.4 9.7 %multiply_convert_fusion = bf16[8,1024,512]{2,1,0:T(8,128)(2,1)S(1)} fusion(f32[8,1024,512]{2,1,0:T(8,128)} %get-tuple-element.44, f32[512]{0:T(512)S(1)} %get-tuple-element.36, f32[512]{0:T(512)S(1)} %rsqrt_multiply_fusion, f32[512]{0:T(512)S(1)} %broadcast_multiply_fusion.1), kind=kLoop, calls=%fused_computation.68 | loop fusion | flops 33554432 | bytes 25171968 | tf_op jit(solution)/shard_map/convert_element_type | solution.py:76
  497.1 8.6 %bitcast_add_fusion = f32[8192,512]{1,0:T(8,128)} fusion(bf16[8,1024,512]{2,1,0:T(8,128)(2,1)S(1)} %bitcast.9, bf16[8192,512]{1,0:T(8,128)(2,1)S(1)} %bitcast.10, bf16[512,512]{1,0:T(8,128)(2,1)S(1)} %copy-done.1, f32[512]{0:T(512)S(1)} %get-tuple-element.39), kind=kOutput, calls=%fused_computation.67 | convolution fusion | flops 4307550208 | bytes 34080768 | tf_op jit(solution)/shard_map/dot_general | solution.py:33
  (54 shorter events, 2.8 us)
Async XLA Ops:
  6.5 11.3 %copy-start.8 = (f32[16]{0:T(128)S(1)}, f32[16]{0:T(128)}, u32[]{:S(2)}) copy-start(f32[16]{0:T(128)} %param.11) | copy-start | bytes 196
  6.5 11.5 %copy-start.9 = (f32[16]{0:T(128)S(1)}, f32[16]{0:T(128)}, u32[]{:S(2)}) copy-start(f32[16]{0:T(128)} %param.12) | copy-start | bytes 196
  6.5 11.7 %copy-start.10 = (f32[32]{0:T(128)S(1)}, f32[32]{0:T(128)}, u32[]{:S(2)}) copy-start(f32[32]{0:T(128)} %param.14) | copy-start | bytes 388
  6.5 269.3 %all-gather.2.cloned.1.call-start = ((), (), s32[]{:S(2)}) async-start(), calls=%async_computation | async-start | bytes 1081344 | tf_op jit(solution)/shard_map/all_gather | solution.py:52
  7.3 63.7 %copy-start.3 = (f32[16,31]{1,0:T(8,128)S(1)}, f32[16,31]{1,0:T(8,128)}, u32[]{:S(2)}) copy-start(f32[16,31]{1,0:T(8,128)} %param.15) | copy-start | bytes 5956
  11.9 132.0 %copy-start.2 = (bf16[16,512]{1,0:T(8,128)(2,1)S(1)}, bf16[16,512]{1,0:T(8,128)(2,1)}, u32[]{:S(2)}) copy-start(bf16[16,512]{1,0:T(8,128)(2,1)} %param.18) | copy-start | bytes 49156
  11.9 206.8 %copy-start.11 = (f32[16]{0:T(128)S(1)}, f32[16]{0:T(128)}, u32[]{:S(2)}) copy-start(f32[16]{0:T(128)} %param.16) | copy-start | bytes 196
  11.9 207.2 %copy-start.12 = (f32[16]{0:T(128)S(1)}, f32[16]{0:T(128)}, u32[]{:S(2)}) copy-start(f32[16]{0:T(128)} %param.17) | copy-start | bytes 196
  11.9 208.1 %copy-start.13 = (f32[16]{0:T(128)S(1)}, f32[16]{0:T(128)}, u32[]{:S(2)}) copy-start(f32[16]{0:T(128)} %param.19) | copy-start | bytes 196
  66.5 3.2 copy-start
  66.6 154.8 %collective-permute-start = (bf16[8,15,512]{2,1,0:T(8,128)(2,1)S(1)}, bf16[8,15,512]{2,1,0:T(8,128)(2,1)S(1)}, u32[]{:S(2)}, u32[]{:S(2)}) collective-permute-start(bf16[8,15,512]{2,1,0:T(8,128)(2,1)S(1)} %get-tuple-element.46), channel_id=1, source_target_pairs={{0,4},{4,8},{8,12},{12,16},{16,20},{20,24},{24,28},{1,5},{5,9},{9,... | collective-permute-start | bytes 368648 | tf_op jit(solution)/shard_map/ppermute | solution.py:17
  69.7 151.6 %collective-permute-start.1 = (bf16[8,15,512]{2,1,0:T(8,128)(2,1)S(1)}, bf16[8,15,512]{2,1,0:T(8,128)(2,1)S(1)}, u32[]{:S(2)}, u32[]{:S(2)}) collective-permute-start(bf16[8,15,512]{2,1,0:T(8,128)(2,1)S(1)} %get-tuple-element.45), channel_id=1, source_target_pairs={{4,0},{8,4},{12,8},{16,12},{20,16},{24,20},{28,24},{5,1},{9,5},{13... | collective-permute-start | bytes 368648 | tf_op jit(solution)/shard_map/ppermute | solution.py:19
  219.1 0.9 copy-start.4
  219.4 56.5 %copy-start.6 = (f32[512]{0:T(512)}, f32[512]{0:T(512)S(1)}, u32[]{:S(2)}) copy-start(f32[512]{0:T(512)S(1)} %dynamic-update-slice.4) | copy-start | bytes 6148
  400.0 47.0 %copy-start.5 = (f32[512]{0:T(512)S(1)}, f32[512]{0:T(512)}, u32[]{:S(2)}) copy-start(f32[512]{0:T(512)} %copy-done.4) | copy-start | bytes 6148
  400.0 47.0 %copy-start.7 = (f32[512]{0:T(512)S(1)}, f32[512]{0:T(512)}, u32[]{:S(2)}) copy-start(f32[512]{0:T(512)} %copy-done.6) | copy-start | bytes 6148
  447.1 50.0 %copy-start.1 = (bf16[512,512]{1,0:T(8,128)(2,1)S(1)}, bf16[512,512]{1,0:T(8,128)(2,1)}, u32[]{:S(2)}) copy-start(bf16[512,512]{1,0:T(8,128)(2,1)} %all_gather.34) | copy-start | bytes 1572868
  487.4 9.7 %slice-start = ((s8[8388608]{0:T(1024)(128)(4,1)}), s8[4194304]{0:T(1024)(128)(4,1)S(1)}, s32[]{:S(2)}) async-start(s8[8388608]{0:T(1024)(128)(4,1)} %bitcast.8), calls=%async_computation.1 | async-start | bytes 8388608
  487.4 9.7 %slice-start.1 = ((s8[8388608]{0:T(1024)(128)(4,1)}), s8[4194304]{0:T(1024)(128)(4,1)S(1)}, s32[]{:S(2)}) async-start(s8[8388608]{0:T(1024)(128)(4,1)} %bitcast.8), calls=%async_computation.2 | async-start | bytes 8388608
Sparse Core Ops, SparseCore 0:
  10.3 56.6 all-gather.1
where the time goes:
time: 514 us; the launch traced here: 513 us
  blocking collectives  265 us (52%)
  other arithmetic  124 us (24%)
  local copies, waits for them, and re-layouts  79.2 us (15%)
  matrix products  26.9 us (5%)
  between operations  13.7 us (3%)
    unnamed x2, blocking collectives  82.4 us
    all_gather x1, blocking collectives, shards(): lax.all_gather(w_out, ('seq', 'batch'), axis=0, tiled=True)  73.1 us
    all_gather x1, blocking collectives, shards(): lax.all_gather(w_depth, ('seq', 'batch'), axis=0, tiled=True)  70.2 us
    reduce_sum x1, other arithmetic, shards(): channel_total = lax.psum(jnp.sum(conv_out, axis=(0, 1)), ('seq', 'batch'))  64.7 us
    concatenate x1, local copies, waits for them, and re-layouts, extended_2(): jnp.concatenate([lax.ppermute(tail, axis, [(i, (i + 1) % count) for i in...  43.7 us
    psum x1, blocking collectives, shards(): channel_total = lax.psum(jnp.sum(conv_out, axis=(0, 1)), ('seq', 'batch'))  39.4 us
    dot_general x2, matrix products, fold_rows(): return jnp.dot(left_rows, piece, preferred_element_type=jnp.float32)  26.9 us
    mul x1, other arithmetic, shards(): hidden[:, :width] * jax.nn.sigmoid(hidden[:, width:])  18.4 us
  transfers between devices with their start and end apart: 3, of which 0 were waited for; matrix products, arithmetic and copies ran while one was open for 15% of the time, Pallas kernels for 0%

commit v1 on v0

v1 whole, which is shorter than its diff:
```python
import functools

import jax
import jax.numpy as jnp
from jax import lax
from jax.experimental import pallas as pl
from jax.experimental.pallas import tpu as pltpu
from jax.sharding import PartitionSpec as P

EPSILON = 1e-05
F32 = jnp.float32
BF16 = jnp.bfloat16
HALO = 16
LANES = 128
VMEM_LIMIT = 60 * 1024 * 1024
SUB = 8
C_LN_GAIN, C_LN_BIAS, C_BN_GAIN, C_BN_BIAS, C_B_OUT, C_B_IN = 0, 1, 2, 3, 4, 5


def bit_stages(seq_size, batch_size):
    stages = []
    for axis, size, low in (("batch", batch_size, 0), ("seq", seq_size, 1)):
        at, top = low, size.bit_length() - 1
        while at < top:
            bits = min(2, top - at)
            stages.append((axis, at, bits))
            at += bits
    if seq_size > 1:
        stages.append(("seq", 0, 1))
    return stages


def gather_relative(block, stages):
    blocks = block[None]
    for axis, shift, bits in stages:
        size = lax.axis_size(axis)
        parts = [blocks]
        for m in range(1, 1 << bits):
            pairs = [(i, i ^ (m << shift)) for i in range(size)]
            parts.append(lax.ppermute(blocks, axis, pairs))
        blocks = jnp.concatenate(parts, axis=0)
    return blocks


def relative_place(seq_xor, batch_xor, stages):
    place, weight = 0, 1
    for axis, shift, bits in stages:
        word = seq_xor if axis == "seq" else batch_xor
        digit = (word >> shift) & ((1 << bits) - 1)
        place = place + digit * weight
        weight <<= bits
    return place


def prep_kernel(stages, seq_size, batch_size, rows, width, half, me_ref, g_ref, wt_ref, wo_ref, p_ref, pt_ref, bb_ref, w_scr):
    seq_me, batch_me = me_ref[0], me_ref[1]
    small = 2 * width
    for s in range(seq_size):
        for b in range(batch_size):
            d = s * batch_size + b
            at = relative_place(seq_me ^ s, batch_me ^ b, stages)
            lo = d * rows
            w_scr[lo : lo + rows, :] = g_ref[at, :, 0:small].astype(F32) * 0.5
            wo_ref[lo : lo + rows, :] = g_ref[at, :, small + LANES :]
            cell = g_ref[at, :, small : small + LANES].astype(F32)
            cell = cell + pltpu.roll(cell, LANES // 2, 1)
            p_ref[lo : lo + rows, :] = cell
            for h in range(2):
                col = cell[:, C_B_IN + h : C_B_IN + h + 1] * 0.5
                bb_ref[2 * lo + h * rows : 2 * lo + (h + 1) * rows, :] = jnp.broadcast_to(col, (rows, LANES))
    for j in range(0, small, 256):
        wt_ref[j : j + 256, :] = w_scr[:, j : j + 256].T.astype(BF16)
    pt_ref[...] = p_ref[...].T


def front_kernel(taps, flags_ref, x_hbm, left_hbm, right_hbm, wt_ref, bb_ref, p_ref, pt_ref, y_ref, st_ref,
                 x_scr, g_scr, y_scr, s_scr, q_scr, sems):
    seqs, frames, width = x_hbm.shape
    step = pl.program_id(0)
    blocks = frames // LANES
    chunk = y_ref.shape[1]
    ext = frames + 2 * HALO

    def copies(s):
        return (
            pltpu.make_async_copy(left_hbm.at[s], x_scr.at[s, pl.ds(0, HALO), :], sems.at[s, 0]),
            pltpu.make_async_copy(x_hbm.at[s], x_scr.at[s, pl.ds(HALO, frames), :], sems.at[s, 1]),
            pltpu.make_async_copy(right_hbm.at[s], x_scr.at[s, pl.ds(HALO + frames, HALO), :], sems.at[s, 2]),
        )

    @pl.when(step == 0)
    def _():
        for s in range(seqs):
            for c in copies(s):
                c.start()
        for s in range(seqs):
            for c in copies(s):
                c.wait()

    gain = pt_ref[C_LN_GAIN : C_LN_GAIN + 1, :]
    bias = pt_ref[C_LN_BIAS : C_LN_BIAS + 1, :]

    def normed(rows):
        rows = rows.astype(F32)
        centre = jnp.mean(rows, axis=-1, keepdims=True)
        rows = rows - centre
        spread = jnp.mean(rows * rows, axis=-1, keepdims=True)
        return (rows * lax.rsqrt(spread + EPSILON) * gain + bias).astype(BF16)

    def gated(rows):
        hid = lax.dot_general(wt_ref[...], rows, (((1,), (1,)), ((), ())), preferred_element_type=F32)
        n = hid.shape[1] // LANES
        add = jnp.concatenate([bb_ref[...]] * n, axis=1)
        hid = hid + add
        val = hid[:width]
        return val + val * jnp.tanh(hid[width:])

    @pl.when(step < blocks)
    def _():
        at = pl.multiple_of(step * LANES, LANES)
        edge = jnp.where(step == 0, HALO * flags_ref[0], 0)
        for s in range(0, seqs, 2):
            rows = jnp.concatenate([x_scr[s, pl.ds(at, LANES), :], x_scr[s + 1, pl.ds(at, LANES), :]], axis=0)
            glu = gated(normed(rows))
            lane = lax.broadcasted_iota(jnp.int32, (1, LANES), 1)
            keep = lane >= edge
            for h in range(2):
                g_scr[pl.ds(pl.multiple_of((step * seqs + s + h) * width, width), width), :] = jnp.where(
                    keep, glu[:, h * LANES : (h + 1) * LANES], 0.0
                )

    @pl.when(step == blocks)
    def _():
        tail = 2 * HALO
        rows = jnp.concatenate([x_scr[s, frames:ext, :] for s in range(seqs)], axis=0)
        glu = gated(normed(rows))
        lane = lax.broadcasted_iota(jnp.int32, (1, LANES), 1)
        keep = lane < tail - HALO * flags_ref[1]
        per = LANES // tail
        for s in range(seqs):
            part = glu[:, (s // per) * LANES : (s // per + 1) * LANES]
            move = (s % per) * tail
            if move:
                part = pltpu.roll(part, LANES - move, 1)
            to = (blocks * seqs + s) * width
            g_scr[to : to + width, :] = jnp.where(keep, part, 0.0)

    @pl.when(step > blocks)
    def _():
        base = (step - blocks - 1) * chunk
        lane = lax.broadcasted_iota(jnp.int32, (SUB, LANES), 1)
        row = lax.broadcasted_iota(jnp.int32, (SUB, LANES), 0)
        reach = 4

        def channel(local):
            c = base + local
            g = g_scr[pl.ds(c, seqs * (blocks + 1), stride=width), :]
            left = g[: seqs * blocks].astype(BF16)
            right = g[seqs:].astype(BF16)
            rows = jnp.concatenate([left, right], axis=1)
            tap = jnp.broadcast_to(p_ref[pl.ds(c, 1), :], (SUB, LANES))
            tap = jnp.where(lane >= LANES - taps, tap, 0.0)
            first = pltpu.roll(tap, 0, 1, stride=1, stride_axis=0)
            low, high = [], []
            for k in range(LANES // SUB):
                f = first if k == 0 else pltpu.roll(first, SUB * k, 1)
                if k < reach:
                    under = lane < row + SUB * k
                    low.append(jnp.where(under, f, 0.0))
                    high.append(jnp.where(under, 0.0, f))
                else:
                    low.append(f)
            zero = jnp.zeros((LANES - reach * SUB, LANES), F32)
            band = jnp.concatenate(low + high + [zero], axis=0).astype(BF16)
            y = jnp.dot(rows, band, preferred_element_type=F32)
            y_scr[pl.ds(local, seqs * blocks, stride=chunk), :] = y
            parts = y.reshape(blocks, seqs, LANES)
            s_scr[pl.ds(c, 1), :] = jnp.sum(jnp.sum(parts, axis=0), axis=0, keepdims=True)
            q_scr[pl.ds(c, 1), :] = jnp.sum(jnp.sum(parts * parts, axis=0), axis=0, keepdims=True)

        unroll = 8

        @pl.loop(0, chunk // unroll)
        def _(i):
            for u in range(unroll):
                channel(i * unroll + u)

        y_ref[...] = y_scr[...].reshape(y_ref.shape).astype(BF16)

    @pl.when(step == pl.num_programs(0) - 1)
    def _():
        total = jnp.sum(s_scr[...].T, axis=0, keepdims=True)
        square = jnp.sum(q_scr[...].T, axis=0, keepdims=True)
        both = jnp.concatenate([total, square], axis=0)
        st_ref[...] = jnp.broadcast_to(both[None], st_ref.shape)


def back_kernel(count, st_ref, p_ref, pt_ref, y_ref, x_ref, wo_ref, o_ref, scale_scr, shift_scr):
    width = wo_ref.shape[0]

    @pl.when(pl.program_id(0) == 0)
    def _():
        both = jnp.sum(st_ref[...], axis=0)
        mean = both[0:1] * (1.0 / count)
        var = jnp.maximum(both[1:2] * (1.0 / count) - mean * mean, 0.0)
        scale = pt_ref[C_BN_GAIN : C_BN_GAIN + 1, :] * lax.rsqrt(var + EPSILON)
        shift = pt_ref[C_BN_BIAS : C_BN_BIAS + 1, :] - mean * scale
        scale_scr[...] = jnp.broadcast_to(scale * 0.5, (LANES, width)).T
        shift_scr[...] = jnp.broadcast_to(shift * 0.5, (LANES, width)).T

    out_bias = pt_ref[C_B_OUT : C_B_OUT + 1, :]
    for s in range(y_ref.shape[0]):
        half = y_ref[s].astype(F32) * scale_scr[...] + shift_scr[...]
        act = (half + half * jnp.tanh(half)).astype(BF16)
        proj = lax.dot_general(act, wo_ref[...], (((0,), (0,)), ((), ())), preferred_element_type=F32)
        o_ref[s] = proj + out_bias + x_ref[s].astype(F32)


def shards(inputs, ln_gain, ln_bias, w_in, b_in, w_depth, bn_gain, bn_bias, w_out, b_out):
    seqs, frames, width = inputs.shape
    rows, taps = w_depth.shape
    seq_size, batch_size = lax.axis_size("seq"), lax.axis_size("batch")
    devices = seq_size * batch_size
    seq_me, batch_me = lax.axis_index("seq"), lax.axis_index("batch")
    half = LANES // 2
    stages = bit_stages(seq_size, batch_size)

    small = jnp.concatenate(
        [jnp.stack([ln_gain, ln_bias, bn_gain, bn_bias, b_out], axis=1),
         b_in.reshape(2, rows).T,
         jnp.zeros((rows, half - 7 - taps), F32),
         w_depth[:, ::-1]], axis=1)
    high = lax.reduce_precision(small, 8, 7)
    low = small - high
    packed = jnp.concatenate([w_in, high.astype(BF16), low.astype(BF16), w_out], axis=1)
    gathered = gather_relative(packed, stages)

    ends = seq_size - 1
    left = lax.ppermute(inputs[:, frames - HALO :], "seq", [(i, i + 1) for i in range(ends)])
    right = lax.ppermute(inputs[:, :HALO], "seq", [(i + 1, i) for i in range(ends)])

    me = jnp.stack([seq_me, batch_me]).astype(jnp.int32)
    if rows % 16:
        order = jnp.stack([relative_place(seq_me ^ (d // batch_size), batch_me ^ (d % batch_size), stages) for d in range(devices)])
        flat = jnp.take(gathered, order, axis=0)
        bias_cells = flat[:, :, 2 * width : 2 * width + LANES].astype(F32)
        bias_cells = (bias_cells[:, :, C_B_IN : C_B_IN + 2] + bias_cells[:, :, half + C_B_IN : half + C_B_IN + 2])
        flat = flat.reshape(1, width, -1)
        pieces = (1, 1)
        me = jnp.zeros((2,), jnp.int32)
    else:
        flat, pieces = gathered, (seq_size, batch_size)
    block_rows = width // (pieces[0] * pieces[1])
    wt, wo, p, pt, bb = pl.pallas_call(
        functools.partial(prep_kernel, stages if pieces[0] > 1 else [], *pieces, block_rows, width, half),
        out_shape=(
            jax.ShapeDtypeStruct((2 * width, width), BF16),
            jax.ShapeDtypeStruct((width, width), BF16),
            jax.ShapeDtypeStruct((width, LANES), F32),
            jax.ShapeDtypeStruct((LANES, width), F32),
            jax.ShapeDtypeStruct((2 * width, LANES), F32),
        ),
        in_specs=[pl.BlockSpec(memory_space=pltpu.SMEM), pl.BlockSpec(memory_space=pltpu.VMEM)],
        out_specs=[pl.BlockSpec(memory_space=pltpu.VMEM)] * 5,
        scratch_shapes=[pltpu.VMEM((width, 2 * width), F32)],
        compiler_params=pltpu.CompilerParams(vmem_limit_bytes=VMEM_LIMIT),
        name="prep",
    )(me, flat)
    if rows % 16:
        bb = jnp.broadcast_to(bias_cells.transpose(0, 2, 1).reshape(2 * width, 1) * 0.5, (2 * width, LANES))

    blocks = frames // LANES
    chunk = 32
    flags = jnp.stack([seq_me == 0, seq_me == ends]).astype(jnp.int32)
    steps = blocks + 1 + width // chunk
    y, st = pl.pallas_call(
        functools.partial(front_kernel, taps),
        grid=(steps,),
        out_shape=(
            jax.ShapeDtypeStruct((seqs * blocks, width, LANES), BF16),
            jax.ShapeDtypeStruct((devices, 2, width), F32),
        ),
        in_specs=[
            pl.BlockSpec(memory_space=pltpu.SMEM),
            pl.BlockSpec(memory_space=pl.ANY),
            pl.BlockSpec(memory_space=pl.ANY),
            pl.BlockSpec(memory_space=pl.ANY),
        ] + [pl.BlockSpec(memory_space=pltpu.VMEM)] * 4,
        out_specs=[
            pl.BlockSpec((seqs * blocks, chunk, LANES), lambda i: (0, jnp.maximum(i - blocks - 1, 0), 0)),
            pl.BlockSpec((devices, 2, width), lambda i: (0, 0, 0)),
        ],
        scratch_shapes=[
            pltpu.VMEM((seqs, frames + 2 * HALO, width), BF16),
            pltpu.VMEM(((blocks + 1) * seqs * width, LANES), F32),
            pltpu.VMEM((seqs * blocks * chunk, LANES), F32),
            pltpu.VMEM((width, LANES), F32),
            pltpu.VMEM((width, LANES), F32),
            pltpu.SemaphoreType.DMA((seqs, 3)),
        ],
        compiler_params=pltpu.CompilerParams(vmem_limit_bytes=VMEM_LIMIT),
        name="front",
    )(flags, inputs, left, right, wt, bb, p, pt)

    st = lax.all_to_all(st, ("seq", "batch"), 0, 0)

    count = float(seqs * frames * devices)
    group = 4
    per = seqs // group
    return pl.pallas_call(
        functools.partial(back_kernel, count),
        grid=(blocks * per,),
        out_shape=jax.ShapeDtypeStruct((seqs, frames, width), F32),
        in_specs=[
            pl.BlockSpec((devices, 2, width), lambda i: (0, 0, 0)),
            pl.BlockSpec((width, LANES), lambda i: (0, 0)),
            pl.BlockSpec((LANES, width), lambda i: (0, 0)),
            pl.BlockSpec((group, width, LANES), lambda i: (i, 0, 0)),
            pl.BlockSpec((group, LANES, width), lambda i: (i % per, i // per, 0)),
            pl.BlockSpec((width, width), lambda i: (0, 0)),
        ],
        out_specs=pl.BlockSpec((group, LANES, width), lambda i: (i % per, i // per, 0)),
        scratch_shapes=[pltpu.VMEM((width, LANES), F32), pltpu.VMEM((width, LANES), F32)],
        compiler_params=pltpu.CompilerParams(vmem_limit_bytes=VMEM_LIMIT),
        name="back",
    )(st, p, pt, y, inputs, wo)


def solution(mesh):
    channel = P(("seq", "batch"))
    matrix = P(("seq", "batch"), None)
    return jax.shard_map(
        shards,
        mesh=mesh,
        in_specs=(
            P("batch", "seq", None), channel, channel, matrix, channel, matrix, channel, channel, matrix, channel,
        ),
        out_specs=P("batch", "seq", None),
        check_vma=False,
    )
```

time: 514 us -> 135 us (0.26)
  blocking collectives: 265 us -> 14 us
  other arithmetic: 124 us -> 1.3 us
  Pallas kernels: 0 us -> 81.2 us
  local copies, waits for them, and re-layouts: 79.2 us -> 13.8 us
  matrix products: 26.9 us -> 0 us
  between operations: 13.7 us -> 0.09 us
  starting transfers between devices: 3.03 us -> 13.6 us
  waiting for transfers between devices: 0.72 us -> 10.1 us
    all_gather x2 -> x0, blocking collectives: 143 us -> none  [the longest x1 73.1 us: shards(): lax.all_gather(w_out, ('seq', 'batch'), axis=0, tiled=True)]
    reduce_sum x4 -> x0, other arithmetic: 82.7 us -> none  [the longest x1 64.7 us: shards(): channel_total = lax.psum(jnp.sum(conv_out, axis=(0, 1)), ('seq', 'batch'))]
    unnamed x2 -> x0, blocking collectives: 82.4 us -> none
    pallas_call x0 -> x3, Pallas kernels: none -> 81.2 us  [the longest x1 56.2 us: shards(): pl.pallas_call(functools.partial(front_kernel, taps), grid=(steps,), out_...]
    concatenate x1 -> x4, local copies, waits for them, and re-layouts: 43.7 us -> 1.75 us  [the longest x1 0.85 us: shards(): jnp.concatenate([w_in, high.astype(BF16), low.astype(BF16), w_out], axis=1)]
    psum x1 -> x0, blocking collectives: 39.4 us -> none  [shards(): channel_total = lax.psum(jnp.sum(conv_out, axis=(0, 1)), ('seq', 'batch'))]
    dot_general x2 -> x0, matrix products: 26.9 us -> none  [fold_rows(): return jnp.dot(left_rows, piece, preferred_element_type=jnp.float32)]
    reshape x2, local copies, waits for them, and re-layouts: 26.2 us -> 0.82 us  [shards(): b_in.reshape(2, rows)]
  transfers between devices with their start and end apart: 3 -> 9, of which waited for: 0 -> 3; matrix products, arithmetic and copies ran while one was open for 15% -> 5% of each run, Pallas kernels for 0% -> 4%
where the time goes in v1:
time: 135 us; the launch traced here: 134 us
  Pallas kernels  81.2 us (60%)
  blocking collectives  14 us (10%)
  local copies, waits for them, and re-layouts  13.8 us (10%)
  starting transfers between devices  13.6 us (10%)
  waiting for transfers between devices  10.1 us (7%)
    pallas_call x1, Pallas kernels, shards(): pl.pallas_call(functools.partial(front_kernel, taps), grid=(steps,), out_...  56.2 us
    pallas_call x1, Pallas kernels, shards(): pl.pallas_call(functools.partial(back_kernel, count), grid=(blocks * per,...  20.1 us
    all_to_all x1, blocking collectives, shards(): st = lax.all_to_all(st, ('seq', 'batch'), 0, 0)  14 us
    ppermute x7, waiting for transfers between devices, gather_relative(): parts.append(lax.ppermute(blocks, axis, pairs))  10.1 us
    ppermute x7, starting transfers between devices, gather_relative(): parts.append(lax.ppermute(blocks, axis, pairs))  9.24 us
    unnamed x12, local copies, waits for them, and re-layouts  5.81 us
    pallas_call x1, Pallas kernels, shards(): pl.pallas_call(functools.partial(prep_kernel, stages if pieces[0] > 1 els...  4.83 us
    another operation x5, local copies, waits for them, and re-layouts, shards(): jnp.stack([ln_gain, ln_bias, bn_gain, bn_bias, b_out], axis=1)  3.66 us
  transfers between devices with their start and end apart: 9, of which 3 were waited for; matrix products, arithmetic and copies ran while one was open for 5% of the time, Pallas kernels for 4%

profile of v1, /device:TPU:0, one launch (start us, length us, event | category | flops | bytes accessed | tf_op | source)
XLA Modules:
  0.0 134.1 jit_solution(18263200621382093561)
XLA Ops:
  0.0 0.7 reshape.3
  0.8 0.7 copy.12
  1.6 0.7 copy.13
  2.3 0.8 rev.3
  3.1 0.7 copy.14
  3.8 0.7 copy.15
  4.5 0.7 copy.16
  5.3 0.8 concatenate.18
  6.2 5.0 %collective-permute-start.4 = (bf16[1,16,1664]{2,1,0:T(8,128)(2,1)S(1)}, bf16[1,16,1664]{2,1,0:T(8,128)(2,1)S(1)}, u32[]{:S(2)}, u32[]{:S(2)}) collective-permute-start(bf16[1,16,1664]{2,1,0:T(8,128)(2,1)S(1)} %bitcast.13), channel_id=1, source_target_pairs={{0,3},{1,2},{2,1},{3,0},{4,7},{5,6},{6,5},{7,4},{8,11},{9,10},{10,... | collective-permute-start | bytes 159752 | tf_op jit(solution)/shard_map/ppermute | solution.py:40
  12.5 1.0 collective-permute-done.4
  13.6 2.7 %collective-permute-done.3 = bf16[1,16,1664]{2,1,0:T(8,128)(2,1)S(1)} collective-permute-done((bf16[1,16,1664]{2,1,0:T(8,128)(2,1)S(1)}, bf16[1,16,1664]{2,1,0:T(8,128)(2,1)S(1)}, u32[]{:S(2)}, u32[]{:S(2)}) %collective-permute-start.3) | collective-permute-done | bytes 53280 | tf_op jit(solution)/shard_map/ppermute | solution.py:40
  16.3 2.5 %collective-permute-start.7 = (bf16[4,16,1664]{2,1,0:T(8,128)(2,1)S(1)}, bf16[4,16,1664]{2,1,0:T(8,128)(2,1)S(1)}, u32[]{:S(2)}, u32[]{:S(2)}) collective-permute-start(bf16[4,16,1664]{2,1,0:T(8,128)(2,1)S(1)} %pad_maximum_fusion), channel_id=1, source_target_pairs={{0,24},{4,28},{8,16},{12,20},{16,8},{20,12},{24,0},{28,4},{1,25},{... | collective-permute-start | bytes 638984 | tf_op jit(solution)/shard_map/ppermute | solution.py:40
  21.8 6.3 %collective-permute-done.5 = bf16[4,16,1664]{2,1,0:T(8,128)(2,1)S(1)} collective-permute-done((bf16[4,16,1664]{2,1,0:T(8,128)(2,1)S(1)}, bf16[4,16,1664]{2,1,0:T(8,128)(2,1)S(1)}, u32[]{:S(2)}, u32[]{:S(2)}) %collective-permute-start.5) | collective-permute-done | bytes 213024 | tf_op jit(solution)/shard_map/ppermute | solution.py:40
  28.1 0.7 constant_dynamic-update-slice_fusion.2
  28.8 0.7 constant_dynamic-update-slice_fusion.1
  29.5 0.7 constant_dynamic-update-slice_fusion
  30.3 1.0 fusion.1
  31.2 1.3 collective-permute-start.1
  32.5 3.0 %collective-permute-start = (bf16[8,16,512]{2,1,0:T(8,128)(2,1)S(1)}, bf16[8,16,512]{2,1,0:T(8,128)(2,1)S(1)}, u32[]{:S(2)}, u32[]{:S(2)}) collective-permute-start(bf16[8,16,512]{2,1,0:T(8,128)(2,1)S(1)} %get-tuple-element.20), channel_id=1, source_target_pairs={{0,4},{4,8},{8,12},{12,16},{16,20},{20,24},{24,28},{1,5},{5,9},{9,... | collective-permute-start | bytes 393224 | tf_op jit(solution)/shard_map/ppermute | solution.py:239
  37.0 1.2 copy-done
  38.2 4.8 %prep.1 = (bf16[1024,512]{1,0:T(8,128)(2,1)}, bf16[512,512]{1,0:T(8,128)(2,1)}, f32[512,128]{1,0:T(8,128)}, f32[128,512]{1,0:T(8,128)}, f32[1024,128]{1,0:T(8,128)}) custom-call(s32[2]{0:T(128)} %pad_add_fusion.me_ref, bf16[32,16,1664]{2,1,0:T(8,128)(2,1)} %copy-done), custom_call_target="tpu_custom_call" | custom-call | tf_op jit(solution)/shard_map/prep/pallas_call | solution.py:254
  43.7 56.2 %front.1 = (bf16[64,512,128]{2,1,0:T(8,128)(2,1)}, f32[32,2,512]{2,1,0:T(2,128)}) custom-call(s32[2]{0:T(128)} %add_convert_fusion.flags_ref, bf16[8,1024,512]{2,1,0:T(8,128)(2,1)} %x_ref.1, bf16[8,16,512]{2,1,0:T(8,128)(2,1)} %copy-done.2, bf16[8,16,512]{2,1,0:T(8,128)(2,1)} %copy-done.1, bf16[1024,512]{1,0:T(8,128)(2,1)} %get-tuple-element.12.wt_ref, ...), custom_call_target="tpu_custom_call" | custom-call | tf_op jit(solution)/shard_map/front/pallas_call | solution.py:276
  99.9 14.0 %all_to_all.5.st_ref = f32[32,2,512]{2,1,0:T(2,128)} all-to-all(f32[32,2,512]{2,1,0:T(2,128)} %get-tuple-element.16), channel_id=1, replica_groups=mesh['seq'=8,'batch'=4] {'seq','batch'}, dimensions={0} | all-to-all | bytes 262144 | tf_op jit(solution)/shard_map/all_to_all | solution.py:305
  114.0 20.1 %back.1 = f32[8,1024,512]{2,1,0:T(8,128)} custom-call(f32[32,2,512]{2,1,0:T(2,128)} %all_to_all.5.st_ref, f32[512,128]{1,0:T(8,128)} %get-tuple-element.14.p_ref, f32[128,512]{1,0:T(8,128)} %get-tuple-element.15.pt_ref, bf16[64,512,128]{2,1,0:T(8,128)(2,1)} %get-tuple-element.17.y_ref, bf16[8,1024,512]{2,1,0:T(8,128)(2,1)} %x_ref.1, ...), custom_call_target="tpu_custom_call" | custom-call | tf_op jit(solution)/shard_map/back/pallas_call | solution.py:310
  (28 shorter events, 6.5 us)
Async XLA Ops:
  6.2 7.4 %collective-permute-start.4 = (bf16[1,16,1664]{2,1,0:T(8,128)(2,1)S(1)}, bf16[1,16,1664]{2,1,0:T(8,128)(2,1)S(1)}, u32[]{:S(2)}, u32[]{:S(2)}) collective-permute-start(bf16[1,16,1664]{2,1,0:T(8,128)(2,1)S(1)} %bitcast.13), channel_id=1, source_target_pairs={{0,3},{1,2},{2,1},{3,0},{4,7},{5,6},{6,5},{7,4},{8,11},{9,10},{10,... | collective-permute-start | bytes 159752 | tf_op jit(solution)/shard_map/ppermute | solution.py:40
  11.2 5.0 %collective-permute-start.3 = (bf16[1,16,1664]{2,1,0:T(8,128)(2,1)S(1)}, bf16[1,16,1664]{2,1,0:T(8,128)(2,1)S(1)}, u32[]{:S(2)}, u32[]{:S(2)}) collective-permute-start(bf16[1,16,1664]{2,1,0:T(8,128)(2,1)S(1)} %bitcast.14), channel_id=1, source_target_pairs={{0,2},{1,3},{2,0},{3,1},{4,6},{5,7},{6,4},{7,5},{8,10},{9,11},{10,... | collective-permute-start | bytes 159752 | tf_op jit(solution)/shard_map/ppermute | solution.py:40
  11.3 5.0 %collective-permute-start.2 = (bf16[1,16,1664]{2,1,0:T(8,128)(2,1)S(1)}, bf16[1,16,1664]{2,1,0:T(8,128)(2,1)S(1)}, u32[]{:S(2)}, u32[]{:S(2)}) collective-permute-start(bf16[1,16,1664]{2,1,0:T(8,128)(2,1)S(1)} %bitcast.15), channel_id=1, source_target_pairs={{0,1},{1,0},{2,3},{3,2},{4,5},{5,4},{6,7},{7,6},{8,9},{9,8},{10,11... | collective-permute-start | bytes 159752 | tf_op jit(solution)/shard_map/ppermute | solution.py:40
  16.3 13.2 %collective-permute-start.7 = (bf16[4,16,1664]{2,1,0:T(8,128)(2,1)S(1)}, bf16[4,16,1664]{2,1,0:T(8,128)(2,1)S(1)}, u32[]{:S(2)}, u32[]{:S(2)}) collective-permute-start(bf16[4,16,1664]{2,1,0:T(8,128)(2,1)S(1)} %pad_maximum_fusion), channel_id=1, source_target_pairs={{0,24},{4,28},{8,16},{12,20},{16,8},{20,12},{24,0},{28,4},{1,25},{... | collective-permute-start | bytes 638984 | tf_op jit(solution)/shard_map/ppermute | solution.py:40
  18.8 10.0 %collective-permute-start.6 = (bf16[4,16,1664]{2,1,0:T(8,128)(2,1)S(1)}, bf16[4,16,1664]{2,1,0:T(8,128)(2,1)S(1)}, u32[]{:S(2)}, u32[]{:S(2)}) collective-permute-start(bf16[4,16,1664]{2,1,0:T(8,128)(2,1)S(1)} %pad_maximum_fusion), channel_id=1, source_target_pairs={{0,16},{4,20},{8,24},{12,28},{16,0},{20,4},{24,8},{28,12},{1,17},{... | collective-permute-start | bytes 638984 | tf_op jit(solution)/shard_map/ppermute | solution.py:40
  19.3 8.8 %collective-permute-start.5 = (bf16[4,16,1664]{2,1,0:T(8,128)(2,1)S(1)}, bf16[4,16,1664]{2,1,0:T(8,128)(2,1)S(1)}, u32[]{:S(2)}, u32[]{:S(2)}) collective-permute-start(bf16[4,16,1664]{2,1,0:T(8,128)(2,1)S(1)} %pad_maximum_fusion), channel_id=1, source_target_pairs={{0,8},{4,12},{8,0},{12,4},{16,24},{20,28},{24,16},{28,20},{1,9},{5... | collective-permute-start | bytes 638984 | tf_op jit(solution)/shard_map/ppermute | solution.py:40
  30.3 6.6 %collective-permute-start.8 = (bf16[16,16,1664]{2,1,0:T(8,128)(2,1)}, bf16[16,16,1664]{2,1,0:T(8,128)(2,1)S(1)}, u32[]{:S(2)}, u32[]{:S(2)}) collective-permute-start(bf16[16,16,1664]{2,1,0:T(8,128)(2,1)} %get-tuple-element.21), channel_id=1, source_target_pairs={{0,4},{4,0},{8,12},{12,8},{16,20},{20,16},{24,28},{28,24},{1,5},{5... | collective-permute-start | bytes 2555912 | tf_op jit(solution)/shard_map/ppermute | solution.py:40
  31.2 11.8 %collective-permute-start.1 = (bf16[8,16,512]{2,1,0:T(8,128)(2,1)S(1)}, bf16[8,16,512]{2,1,0:T(8,128)(2,1)S(1)}, u32[]{:S(2)}, u32[]{:S(2)}) collective-permute-start(bf16[8,16,512]{2,1,0:T(8,128)(2,1)S(1)} %get-tuple-element.19), channel_id=1, source_target_pairs={{4,0},{8,4},{12,8},{16,12},{20,16},{24,20},{28,24},{5,1},{9,5},{13... | collective-permute-start | bytes 393224 | tf_op jit(solution)/shard_map/ppermute | solution.py:240
  32.5 10.5 %collective-permute-start = (bf16[8,16,512]{2,1,0:T(8,128)(2,1)S(1)}, bf16[8,16,512]{2,1,0:T(8,128)(2,1)S(1)}, u32[]{:S(2)}, u32[]{:S(2)}) collective-permute-start(bf16[8,16,512]{2,1,0:T(8,128)(2,1)S(1)} %get-tuple-element.20), channel_id=1, source_target_pairs={{0,4},{4,8},{8,12},{12,16},{16,20},{20,24},{24,28},{1,5},{5,9},{9,... | collective-permute-start | bytes 393224 | tf_op jit(solution)/shard_map/ppermute | solution.py:239
  37.0 1.2 copy-start
  43.0 0.6 copy-start.1
  43.0 0.7 copy-start.2

commit v2 on v0

v2 whole, which is shorter than its diff:
```python
import functools

import jax
import jax.numpy as jnp
from jax import lax
from jax.experimental import pallas as pl
from jax.experimental.pallas import tpu as pltpu
from jax.sharding import PartitionSpec as P

EPSILON = 1e-05
F32 = jnp.float32
BF16 = jnp.bfloat16
HALO = 16
LANES = 128
FRONT_VMEM = 36 * 1024 * 1024
BACK_VMEM = 16 * 1024 * 1024
SUB = 8
C_LN_GAIN, C_LN_BIAS, C_BN_GAIN, C_BN_BIAS, C_B_OUT, C_B_IN = 0, 1, 2, 3, 4, 5


def bit_stages(seq_size, batch_size):
    stages = []
    for axis, size, low in (("batch", batch_size, 0), ("seq", seq_size, 1)):
        at, top = low, size.bit_length() - 1
        while at < top:
            bits = min(2, top - at)
            stages.append((axis, at, bits))
            at += bits
    if seq_size > 1:
        stages.append(("seq", 0, 1))
    return stages


def gather_relative(block, stages):
    blocks = block[None]
    for axis, shift, bits in stages:
        size = lax.axis_size(axis)
        parts = [blocks]
        for m in range(1, 1 << bits):
            pairs = [(i, i ^ (m << shift)) for i in range(size)]
            parts.append(lax.ppermute(blocks, axis, pairs))
        blocks = jnp.concatenate(parts, axis=0)
    return blocks


def relative_place(seq_xor, batch_xor, stages):
    place, weight = 0, 1
    for axis, shift, bits in stages:
        word = seq_xor if axis == "seq" else batch_xor
        digit = (word >> shift) & ((1 << bits) - 1)
        place = place + digit * weight
        weight <<= bits
    return place


def pack_kernel(taps, ln_gain, ln_bias, w_in, b_in, w_depth, bn_gain, bn_bias, w_out, b_out, o_ref):
    rows, small = w_in.shape
    lane = lax.broadcasted_iota(jnp.int32, (rows, LANES), 1)
    row = lax.broadcasted_iota(jnp.int32, (rows, LANES), 0)

    def column(ref, start=0):
        line = jnp.broadcast_to(ref[...].reshape(1, -1), (rows, ref.shape[0]))
        hit = lane[:, : line.shape[1]] == row[:, : line.shape[1]] + start
        return jnp.sum(jnp.where(hit, line, 0.0), axis=1, keepdims=True)

    cells = (
        (C_LN_GAIN, column(ln_gain)),
        (C_LN_BIAS, column(ln_bias)),
        (C_BN_GAIN, column(bn_gain)),
        (C_BN_BIAS, column(bn_bias)),
        (C_B_OUT, column(b_out)),
        (C_B_IN, column(b_in)),
        (C_B_IN + 1, column(b_in, rows)),
    ) + tuple((LANES // 2 - 1 - k, w_depth[:, k : k + 1]) for k in range(taps))
    cell = jnp.zeros((rows, LANES), F32)
    for at, value in cells:
        cell = jnp.where((lane & (LANES // 2 - 1)) == at, value, cell)
    high = cell.astype(BF16)
    low = (cell - high.astype(F32)).astype(BF16)
    o_ref[:, :small] = w_in[...]
    o_ref[:, small : small + LANES] = jnp.where(lane < LANES // 2, high.astype(F32), low.astype(F32)).astype(BF16)
    o_ref[:, small + LANES :] = w_out[...]


def front_kernel(taps, stages, seq_size, batch_size, where_ref, flat_ref, x_ref, left_ref, right_ref,
                 y_ref, st_ref, wo_ref, pt_ref,
                 w_scr, wt_scr, bb_scr, p_scr, g_scr, y_scr, s_scr, q_scr):
    seqs, frames, width = x_ref.shape
    blocks = frames // LANES
    chunk = y_scr.shape[0] // (seqs * blocks)
    small = 2 * width
    rows = width // (seq_size * batch_size)
    seq_me, batch_me = where_ref[0], where_ref[1]
    first_edge, last_edge = where_ref[2], where_ref[3]

    for s in range(seq_size):
        for b in range(batch_size):
            lo = (s * batch_size + b) * rows
            at = relative_place(seq_me ^ s, batch_me ^ b, stages)
            w_scr[lo : lo + rows, :] = flat_ref[at, :, 0:small].astype(F32) * 0.5
            wo_ref[lo : lo + rows, :] = flat_ref[at, :, small + LANES :]
            cell = flat_ref[at, :, small : small + LANES].astype(F32)
            cell = cell + pltpu.roll(cell, LANES // 2, 1)
            p_scr[lo : lo + rows, :] = cell
            for h in range(2):
                col = cell[:, C_B_IN + h : C_B_IN + h + 1] * 0.5
                bb_scr[2 * lo + h * rows : 2 * lo + (h + 1) * rows, :] = jnp.broadcast_to(col, (rows, LANES))
    for j in range(0, small, 256):
        wt_scr[j : j + 256, :] = w_scr[:, j : j + 256].T.astype(BF16)
    pt_ref[...] = p_scr[...].T

    gain = pt_ref[C_LN_GAIN : C_LN_GAIN + 1, :]
    bias = pt_ref[C_LN_BIAS : C_LN_BIAS + 1, :]

    def normed(part):
        part = part.astype(F32)
        centre = jnp.mean(part, axis=-1, keepdims=True)
        part = part - centre
        spread = jnp.mean(part * part, axis=-1, keepdims=True)
        return (part * lax.rsqrt(spread + EPSILON) * gain + bias).astype(BF16)

    def gated(part):
        hid = lax.dot_general(wt_scr[...], part, (((1,), (1,)), ((), ())), preferred_element_type=F32)
        add = jnp.concatenate([bb_scr[...]] * (hid.shape[1] // LANES), axis=1)
        hid = hid + add
        val = hid[:width]
        return val + val * jnp.tanh(hid[width:])

    lane = lax.broadcasted_iota(jnp.int32, (1, LANES), 1)

    def block(b, piece, edge):
        for s in range(0, seqs, 2):
            glu = gated(normed(jnp.concatenate([piece(s), piece(s + 1)], axis=0)))
            for h in range(2):
                part = glu[:, h * LANES : (h + 1) * LANES]
                if edge is not None:
                    part = jnp.where(lane >= edge, part, 0.0)
                to = (b * seqs + s + h) * width
                g_scr[pl.ds(to if isinstance(b, int) else pl.multiple_of(to, width), width), :] = part

    block(0, lambda s: jnp.concatenate([left_ref[s], x_ref[s, : LANES - HALO, :]], axis=0), HALO * first_edge)

    @pl.loop(1, blocks)
    def _(b):
        at = pl.multiple_of(b * LANES - HALO, HALO)
        block(b, lambda s: x_ref[s, pl.ds(at, LANES), :], None)

    tail = 2 * HALO
    ends = []
    for s in range(seqs):
        ends += [x_ref[s, frames - HALO :, :], right_ref[s]]
    glu = gated(normed(jnp.concatenate(ends, axis=0)))
    per = LANES // tail
    for s in range(seqs):
        part = glu[:, (s // per) * LANES : (s // per + 1) * LANES]
        move = (s % per) * tail
        if move:
            part = pltpu.roll(part, LANES - move, 1)
        to = (blocks * seqs + s) * width
        g_scr[to : to + width, :] = jnp.where(lane < tail - HALO * last_edge, part, 0.0)

    wide = lax.broadcasted_iota(jnp.int32, (SUB, LANES), 1)
    row = lax.broadcasted_iota(jnp.int32, (SUB, LANES), 0)
    reach = 4

    def channel(c, local):
        g = g_scr[pl.ds(c, seqs * (blocks + 1), stride=width), :]
        pair = jnp.concatenate([g[: seqs * blocks].astype(BF16), g[seqs:].astype(BF16)], axis=1)
        tap = jnp.broadcast_to(p_scr[pl.ds(c, 1), :], (SUB, LANES))
        tap = jnp.where(wide >= LANES - taps, tap, 0.0)
        first = pltpu.roll(tap, 0, 1, stride=1, stride_axis=0)
        low, high = [], []
        for k in range(LANES // SUB):
            f = first if k == 0 else pltpu.roll(first, SUB * k, 1)
            if k < reach:
                under = wide < row + SUB * k
                low.append(jnp.where(under, f, 0.0))
                high.append(jnp.where(under, 0.0, f))
            else:
                low.append(f)
        zero = jnp.zeros((LANES - reach * SUB, LANES), F32)
        band = jnp.concatenate(low + high + [zero], axis=0).astype(BF16)
        y = jnp.dot(pair, band, preferred_element_type=F32)
        y_scr[pl.ds(local, seqs * blocks, stride=chunk), :] = y
        parts = y.reshape(blocks, seqs, LANES)
        s_scr[pl.ds(c, 1), :] = jnp.sum(jnp.sum(parts, axis=0), axis=0, keepdims=True)
        q_scr[pl.ds(c, 1), :] = jnp.sum(jnp.sum(parts * parts, axis=0), axis=0, keepdims=True)

    unroll = 16

    @pl.loop(0, width // chunk)
    def _(n):
        base = pl.multiple_of(n * chunk, chunk)

        @pl.loop(0, chunk // unroll)
        def _(i):
            for u in range(unroll):
                local = i * unroll + u
                channel(base + local, local)

        y_ref[:, pl.ds(base, chunk), :] = y_scr[...].reshape(seqs * blocks, chunk, LANES).astype(BF16)

    total = jnp.sum(s_scr[...].T, axis=0, keepdims=True)
    square = jnp.sum(q_scr[...].T, axis=0, keepdims=True)
    st_ref[...] = jnp.broadcast_to(jnp.concatenate([total, square], axis=0)[None], st_ref.shape)


def back_kernel(count, st_ref, pt_ref, y_ref, x_ref, wo_ref, o_hbm, scale_scr, shift_scr, o_scr, sems):
    seqs, frames, width = x_ref.shape
    blocks = frames // LANES
    group = o_scr.shape[1]
    per = seqs // group
    both = jnp.sum(st_ref[...], axis=0)
    mean = both[0:1] * (1.0 / count)
    var = jnp.maximum(both[1:2] * (1.0 / count) - mean * mean, 0.0)
    scale = pt_ref[C_BN_GAIN : C_BN_GAIN + 1, :] * lax.rsqrt(var + EPSILON)
    shift = pt_ref[C_BN_BIAS : C_BN_BIAS + 1, :] - mean * scale
    scale_scr[...] = jnp.broadcast_to(scale * 0.5, (LANES, width)).T
    shift_scr[...] = jnp.broadcast_to(shift * 0.5, (LANES, width)).T
    out_bias = pt_ref[C_B_OUT : C_B_OUT + 1, :]

    def copy(b, p):
        target = o_hbm.at[pl.ds(p * group, group), pl.ds(pl.multiple_of(b * LANES, LANES), LANES), :]
        return pltpu.make_async_copy(o_scr.at[p], target, sems.at[p])

    @pl.loop(0, blocks)
    def _(b):
        for p in range(per):
            acts = []
            for s in range(group):
                half = y_ref[b * seqs + p * group + s].astype(F32) * scale_scr[...] + shift_scr[...]
                acts.append((half + half * jnp.tanh(half)).astype(BF16))
            act = jnp.concatenate(acts, axis=1)
            proj = lax.dot_general(act, wo_ref[...], (((0,), (0,)), ((), ())), preferred_element_type=F32)

            @pl.when(b > 0)
            def _():
                copy(b - 1, p).wait()

            at = pl.multiple_of(b * LANES, LANES)
            for s in range(group):
                rest = x_ref[p * group + s, pl.ds(at, LANES), :].astype(F32) + out_bias
                o_scr[p, s] = proj[LANES * s : LANES * (s + 1)] + rest
            copy(b, p).start()

    for p in range(per):
        copy(blocks - 1, p).wait()


def shards(inputs, ln_gain, ln_bias, w_in, b_in, w_depth, bn_gain, bn_bias, w_out, b_out):
    seqs, frames, width = inputs.shape
    rows, taps = w_depth.shape
    seq_size, batch_size = lax.axis_size("seq"), lax.axis_size("batch")
    devices = seq_size * batch_size
    seq_me, batch_me = lax.axis_index("seq"), lax.axis_index("batch")
    stages = bit_stages(seq_size, batch_size)
    vmem = pl.BlockSpec(memory_space=pltpu.VMEM)
    blocks = frames // LANES

    packed = pl.pallas_call(
        functools.partial(pack_kernel, taps),
        out_shape=jax.ShapeDtypeStruct((rows, 3 * width + LANES), BF16),
        in_specs=[vmem] * 9,
        out_specs=vmem,
        name="pack",
    )(ln_gain, ln_bias, w_in, b_in, w_depth, bn_gain, bn_bias, w_out, b_out)
    ends = seq_size - 1
    left = lax.ppermute(inputs[:, frames - HALO :], "seq", [(i, i + 1) for i in range(ends)])
    right = lax.ppermute(inputs[:, :HALO], "seq", [(i + 1, i) for i in range(ends)])
    flat = gather_relative(packed, stages)

    pieces, at = (seq_size, batch_size), (seq_me, batch_me)
    if rows % 16:
        order = jnp.stack([relative_place(seq_me ^ (d // batch_size), batch_me ^ (d % batch_size), stages) for d in range(devices)])
        flat = jnp.take(flat, order, axis=0)
        for start in (2 * width + C_B_IN, 2 * width + LANES // 2 + C_B_IN):
            cut = flat[:, :, start : start + 2].transpose(0, 2, 1).reshape(2, width).T.reshape(devices, rows, 2)
            flat = lax.dynamic_update_slice(flat, cut, (0, 0, start))
        flat = flat.reshape(1, width, -1)
        pieces, at, stages = (1, 1), (0 * seq_me, 0 * batch_me), []
    place = jnp.stack([*at, seq_me == 0, seq_me == ends]).astype(jnp.int32)

    chunk = 64
    x = pltpu.with_memory_space_constraint(inputs, pltpu.VMEM)
    y, st, wo, pt = pl.pallas_call(
        functools.partial(front_kernel, taps, stages, *pieces),
        out_shape=(
            pltpu.VMEM((seqs * blocks, width, LANES), BF16),
            jax.ShapeDtypeStruct((devices, 2, width), F32),
            pltpu.VMEM((width, width), BF16),
            pltpu.VMEM((LANES, width), F32),
        ),
        in_specs=[pl.BlockSpec(memory_space=pltpu.SMEM)] + [vmem] * 4,
        out_specs=[vmem] * 4,
        scratch_shapes=[
            pltpu.VMEM((width, 2 * width), F32),
            pltpu.VMEM((2 * width, width), BF16),
            pltpu.VMEM((2 * width, LANES), F32),
            pltpu.VMEM((width, LANES), F32),
            pltpu.VMEM(((blocks + 1) * seqs * width, LANES), F32),
            pltpu.VMEM((seqs * blocks * chunk, LANES), F32),
            pltpu.VMEM((width, LANES), F32),
            pltpu.VMEM((width, LANES), F32),
        ],
        compiler_params=pltpu.CompilerParams(vmem_limit_bytes=FRONT_VMEM),
        name="front",
    )(place, flat, x, left, right)

    st = lax.all_to_all(st, ("seq", "batch"), 0, 0)

    group = 4
    y, x, wo, pt = (pltpu.with_memory_space_constraint(a, pltpu.VMEM) for a in (y, x, wo, pt))
    return pl.pallas_call(
        functools.partial(back_kernel, float(seqs * frames * devices)),
        out_shape=jax.ShapeDtypeStruct((seqs, frames, width), F32),
        in_specs=[vmem] * 5,
        out_specs=pl.BlockSpec(memory_space=pl.ANY),
        scratch_shapes=[
            pltpu.VMEM((width, LANES), F32),
            pltpu.VMEM((width, LANES), F32),
            pltpu.VMEM((seqs // group, group, LANES, width), F32),
            pltpu.SemaphoreType.DMA((seqs // group,)),
        ],
        compiler_params=pltpu.CompilerParams(vmem_limit_bytes=BACK_VMEM),
        name="back",
    )(st, pt, y, x, wo)


def solution(mesh):
    channel = P(("seq", "batch"))
    matrix = P(("seq", "batch"), None)
    return jax.shard_map(
        shards,
        mesh=mesh,
        in_specs=(
            P("batch", "seq", None), channel, channel, matrix, channel, matrix, channel, channel, matrix, channel,
        ),
        out_specs=P("batch", "seq", None),
        check_vma=False,
    )
```

time: 514 us -> 111 us (0.22)
  blocking collectives: 265 us -> 16.1 us
  other arithmetic: 124 us -> 0.92 us
  local copies, waits for them, and re-layouts: 79.2 us -> 10.4 us
  Pallas kernels: 0 us -> 59.7 us
  matrix products: 26.9 us -> 0 us
  between operations: 13.7 us -> 0.08 us
  starting transfers between devices: 3.03 us -> 13.5 us
  waiting for transfers between devices: 0.72 us -> 10.3 us
    all_gather x2 -> x0, blocking collectives: 143 us -> none  [the longest x1 73.1 us: shards(): lax.all_gather(w_out, ('seq', 'batch'), axis=0, tiled=True)]
    reduce_sum x4 -> x0, other arithmetic: 82.7 us -> none  [the longest x1 64.7 us: shards(): channel_total = lax.psum(jnp.sum(conv_out, axis=(0, 1)), ('seq', 'batch'))]
    unnamed x2 -> x0, blocking collectives: 82.4 us -> none
    pallas_call x0 -> x3, Pallas kernels: none -> 59.7 us  [the longest x1 44 us: shards(): pl.pallas_call(functools.partial(front_kernel, taps, stages, *pieces), ou...]
    concatenate x1 -> x2, local copies, waits for them, and re-layouts: 43.7 us -> 0.82 us  [gather_relative(): blocks = jnp.concatenate(parts, axis=0)]
    psum x1 -> x0, blocking collectives: 39.4 us -> none  [shards(): channel_total = lax.psum(jnp.sum(conv_out, axis=(0, 1)), ('seq', 'batch'))]
    dot_general x2 -> x0, matrix products: 26.9 us -> none  [fold_rows(): return jnp.dot(left_rows, piece, preferred_element_type=jnp.float32)]
    reshape x2 -> x0, local copies, waits for them, and re-layouts: 26.2 us -> none  [the longest x1 15.4 us: shards(): (hidden[:, :width] * jax.nn.sigmoid(hidden[:, width:])).reshape(seq_count...]
  transfers between devices with their start and end apart: 3 -> 9, of which waited for: 0 -> 4; matrix products, arithmetic and copies ran while one was open for 15% -> 5% of each run, Pallas kernels for 0% -> 0%
where the time goes in v2:
time: 111 us
  Pallas kernels  59.7 us (54%)
  blocking collectives  16.1 us (15%)
  starting transfers between devices  13.5 us (12%)
  local copies, waits for them, and re-layouts  10.4 us (9%)
  waiting for transfers between devices  10.3 us (9%)
    pallas_call x1, Pallas kernels, shards(): pl.pallas_call(functools.partial(front_kernel, taps, stages, *pieces), ou...  44 us
    all_to_all x1, blocking collectives, shards(): st = lax.all_to_all(st, ('seq', 'batch'), 0, 0)  16.1 us
    pallas_call x1, Pallas kernels, shards(): pl.pallas_call(functools.partial(back_kernel, float(seqs * frames * devic...  14 us
    ppermute x7, waiting for transfers between devices, gather_relative(): parts.append(lax.ppermute(blocks, axis, pairs))  9.55 us
    ppermute x7, starting transfers between devices, gather_relative(): parts.append(lax.ppermute(blocks, axis, pairs))  9.17 us
    unnamed x10, local copies, waits for them, and re-layouts  8.6 us
    ppermute x1, starting transfers between devices, shards(): lax.ppermute(inputs[:, frames - HALO:], 'seq', [(i, i + 1) for i in range...  3.05 us
  transfers between devices with their start and end apart: 9, of which 4 were waited for; matrix products, arithmetic and copies ran while one was open for 5% of the time, Pallas kernels for 0%

profile of v2, /device:TPU:0, one launch (start us, length us, event | category | flops | bytes accessed | tf_op | source)
XLA Modules:
  0.0 111.0 jit_solution(5225208054698753000)
XLA Ops:
  0.0 1.7 %pack.1 = bf16[16,1664]{1,0:T(8,128)(2,1)} custom-call(f32[16]{0:T(128)} %ln_gain.1, f32[16]{0:T(128)} %ln_bias.1, bf16[16,1024]{1,0:T(8,128)(2,1)} %w_in.1, f32[32]{0:T(128)} %b_in.1, f32[16,31]{1,0:T(8,128)} %w_depth.1, f32[16]{0:T(128)} %bn_gain.1, f32[16]{0:T(128)} %bn_bias.1, bf16[16,512]{1,0:T(8,128)(2,1)} %w_out.1, f32[16]{0:T(128)} %b_out.1), custom_call_target="tpu_custom_call" | custom-call | tf_op jit(solution)/shard_map/pack/pallas_call | solution.py:260
  1.7 5.0 %collective-permute-start.2 = (bf16[1,16,1664]{2,1,0:T(8,128)(2,1)}, bf16[1,16,1664]{2,1,0:T(8,128)(2,1)S(1)}, u32[]{:S(2)}, u32[]{:S(2)}) collective-permute-start(bf16[1,16,1664]{2,1,0:T(8,128)(2,1)} %bitcast.7), channel_id=1, source_target_pairs={{0,3},{1,2},{2,1},{3,0},{4,7},{5,6},{6,5},{7,4},{8,11},{9,10},{10,... | collective-permute-start | bytes 159752 | tf_op jit(solution)/shard_map/ppermute | solution.py:41
  6.7 0.6 collective-permute-start
  7.3 1.5 %constant_dynamic-update-slice_fusion.6 = (bf16[16,16,1664]{2,1,0:T(8,128)(2,1)}, bf16[32,16,1664]{2,1,0:T(8,128)(2,1)S(1)}) fusion(bf16[16,1664]{1,0:T(8,128)(2,1)} %pack.1), kind=kLoop, calls=%fused_computation.7 | loop fusion | bytes 159744
  8.8 0.5 collective-permute-done.2
  9.3 2.7 %collective-permute-done.1 = bf16[1,16,1664]{2,1,0:T(8,128)(2,1)S(1)} collective-permute-done((bf16[1,16,1664]{2,1,0:T(8,128)(2,1)}, bf16[1,16,1664]{2,1,0:T(8,128)(2,1)S(1)}, u32[]{:S(2)}, u32[]{:S(2)}) %collective-permute-start.1) | collective-permute-done | bytes 53280 | tf_op jit(solution)/shard_map/ppermute | solution.py:41
  12.0 0.8 pad_maximum_fusion
  12.8 2.5 %collective-permute-start.5 = (bf16[4,16,1664]{2,1,0:T(8,128)(2,1)S(1)}, bf16[4,16,1664]{2,1,0:T(8,128)(2,1)S(1)}, u32[]{:S(2)}, u32[]{:S(2)}) collective-permute-start(bf16[4,16,1664]{2,1,0:T(8,128)(2,1)S(1)} %pad_maximum_fusion), channel_id=1, source_target_pairs={{0,24},{4,28},{8,16},{12,20},{16,8},{20,12},{24,0},{28,4},{1,25},{... | collective-permute-start | bytes 638984 | tf_op jit(solution)/shard_map/ppermute | solution.py:41
  15.9 0.5 collective-permute-start.3
  16.4 0.6 constant_dynamic-update-slice_fusion.5
  17.0 0.6 constant_dynamic-update-slice_fusion.4
  17.7 0.6 constant_dynamic-update-slice_fusion.3
  18.3 6.3 %collective-permute-done.3 = bf16[4,16,1664]{2,1,0:T(8,128)(2,1)S(1)} collective-permute-done((bf16[4,16,1664]{2,1,0:T(8,128)(2,1)S(1)}, bf16[4,16,1664]{2,1,0:T(8,128)(2,1)S(1)}, u32[]{:S(2)}, u32[]{:S(2)}) %collective-permute-start.3) | collective-permute-done | bytes 213024 | tf_op jit(solution)/shard_map/ppermute | solution.py:41
  24.6 0.7 constant_dynamic-update-slice_fusion.2
  25.3 0.7 constant_dynamic-update-slice_fusion.1
  26.1 0.7 constant_dynamic-update-slice_fusion
  26.8 1.0 fusion
  27.8 1.3 %collective-permute-start.8 = (bf16[8,16,512]{2,1,0:T(8,128)(2,1)S(1)}, bf16[8,16,512]{2,1,0:T(8,128)(2,1)S(1)}, u32[]{:S(2)}, u32[]{:S(2)}) collective-permute-start(bf16[8,16,512]{2,1,0:T(8,128)(2,1)S(1)} %get-tuple-element.13), channel_id=1, source_target_pairs={{4,0},{8,4},{12,8},{16,12},{20,16},{24,20},{28,24},{5,1},{9,5},{13... | collective-permute-start | bytes 393224 | tf_op jit(solution)/shard_map/ppermute | solution.py:269
  29.1 3.0 %collective-permute-start.7 = (bf16[8,16,512]{2,1,0:T(8,128)(2,1)S(1)}, bf16[8,16,512]{2,1,0:T(8,128)(2,1)S(1)}, u32[]{:S(2)}, u32[]{:S(2)}) collective-permute-start(bf16[8,16,512]{2,1,0:T(8,128)(2,1)S(1)} %get-tuple-element.14), channel_id=1, source_target_pairs={{0,4},{4,8},{8,12},{12,16},{16,20},{20,24},{24,28},{1,5},{5,9},{9,... | collective-permute-start | bytes 393224 | tf_op jit(solution)/shard_map/ppermute | solution.py:268
  32.3 0.7 collective-permute-done.7.left_ref
  33.5 3.4 %copy-done = bf16[8,1024,512]{2,1,0:T(8,128)(2,1)S(1)} copy-done((bf16[8,1024,512]{2,1,0:T(8,128)(2,1)S(1)}, bf16[8,1024,512]{2,1,0:T(8,128)(2,1)}, u32[]{:S(2)}) %copy-start) | copy-done | bytes 8388632
  36.9 44.0 %front.1 = (bf16[64,512,128]{2,1,0:T(8,128)(2,1)S(1)}, f32[32,2,512]{2,1,0:T(2,128)S(1)}, bf16[512,512]{1,0:T(8,128)(2,1)S(1)}, f32[128,512]{1,0:T(8,128)S(1)}) custom-call(s32[4]{0:T(128)S(1)} %pad_add_fusion.where_ref, bf16[32,16,1664]{2,1,0:T(8,128)(2,1)} %copy-done.1, bf16[8,1024,512]{2,1,0:T(8,128)(2,1)S(1)} %copy-done, ...), custom_call_target="tpu_custom_call" | custom-call | tf_op jit(solution)/shard_map/front/pallas_call | solution.py:285
  80.9 16.1 %all_to_all.5.st_ref = f32[32,2,512]{2,1,0:T(2,128)S(1)} all-to-all(f32[32,2,512]{2,1,0:T(2,128)S(1)} %get-tuple-element.9), channel_id=1, replica_groups=mesh['seq'=8,'batch'=4] {'seq','batch'}, dimensions={0} | all-to-all | bytes 262144 | tf_op jit(solution)/shard_map/all_to_all | solution.py:309
  97.0 14.0 %back.1 = f32[8,1024,512]{2,1,0:T(8,128)} custom-call(f32[32,2,512]{2,1,0:T(2,128)S(1)} %all_to_all.5.st_ref, f32[128,512]{1,0:T(8,128)S(1)} %get-tuple-element.10.pt_ref, bf16[64,512,128]{2,1,0:T(8,128)(2,1)S(1)} %get-tuple-element.11.y_ref, bf16[8,1024,512]{2,1,0:T(8,128)(2,1)S(1)} %copy-done, bf16[512,512]{1,0:T(8,128)(2,1)S(1)} %get-tuple-element.12.wo_ref), custom_call_target="tpu_custom_call" | custom-call | tf_op jit(solution)/shard_map/back/pallas_call | solution.py:313
  (13 shorter events, 1.1 us)
Async XLA Ops:
  1.7 7.6 %collective-permute-start.2 = (bf16[1,16,1664]{2,1,0:T(8,128)(2,1)}, bf16[1,16,1664]{2,1,0:T(8,128)(2,1)S(1)}, u32[]{:S(2)}, u32[]{:S(2)}) collective-permute-start(bf16[1,16,1664]{2,1,0:T(8,128)(2,1)} %bitcast.7), channel_id=1, source_target_pairs={{0,3},{1,2},{2,1},{3,0},{4,7},{5,6},{6,5},{7,4},{8,11},{9,10},{10,... | collective-permute-start | bytes 159752 | tf_op jit(solution)/shard_map/ppermute | solution.py:41
  6.7 5.2 %collective-permute-start.1 = (bf16[1,16,1664]{2,1,0:T(8,128)(2,1)}, bf16[1,16,1664]{2,1,0:T(8,128)(2,1)S(1)}, u32[]{:S(2)}, u32[]{:S(2)}) collective-permute-start(bf16[1,16,1664]{2,1,0:T(8,128)(2,1)} %bitcast.8), channel_id=1, source_target_pairs={{0,2},{1,3},{2,0},{3,1},{4,6},{5,7},{6,4},{7,5},{8,10},{9,11},{10,... | collective-permute-start | bytes 159752 | tf_op jit(solution)/shard_map/ppermute | solution.py:41
  6.7 5.2 %collective-permute-start = (bf16[1,16,1664]{2,1,0:T(8,128)(2,1)}, bf16[1,16,1664]{2,1,0:T(8,128)(2,1)S(1)}, u32[]{:S(2)}, u32[]{:S(2)}) collective-permute-start(bf16[1,16,1664]{2,1,0:T(8,128)(2,1)} %bitcast.9), channel_id=1, source_target_pairs={{0,1},{1,0},{2,3},{3,2},{4,5},{5,4},{6,7},{7,6},{8,9},{9,8},{10,11... | collective-permute-start | bytes 159752 | tf_op jit(solution)/shard_map/ppermute | solution.py:41
  12.8 13.2 %collective-permute-start.5 = (bf16[4,16,1664]{2,1,0:T(8,128)(2,1)S(1)}, bf16[4,16,1664]{2,1,0:T(8,128)(2,1)S(1)}, u32[]{:S(2)}, u32[]{:S(2)}) collective-permute-start(bf16[4,16,1664]{2,1,0:T(8,128)(2,1)S(1)} %pad_maximum_fusion), channel_id=1, source_target_pairs={{0,24},{4,28},{8,16},{12,20},{16,8},{20,12},{24,0},{28,4},{1,25},{... | collective-permute-start | bytes 638984 | tf_op jit(solution)/shard_map/ppermute | solution.py:41
  15.4 10.0 %collective-permute-start.4 = (bf16[4,16,1664]{2,1,0:T(8,128)(2,1)S(1)}, bf16[4,16,1664]{2,1,0:T(8,128)(2,1)S(1)}, u32[]{:S(2)}, u32[]{:S(2)}) collective-permute-start(bf16[4,16,1664]{2,1,0:T(8,128)(2,1)S(1)} %pad_maximum_fusion), channel_id=1, source_target_pairs={{0,16},{4,20},{8,24},{12,28},{16,0},{20,4},{24,8},{28,12},{1,17},{... | collective-permute-start | bytes 638984 | tf_op jit(solution)/shard_map/ppermute | solution.py:41
  15.9 8.8 %collective-permute-start.3 = (bf16[4,16,1664]{2,1,0:T(8,128)(2,1)S(1)}, bf16[4,16,1664]{2,1,0:T(8,128)(2,1)S(1)}, u32[]{:S(2)}, u32[]{:S(2)}) collective-permute-start(bf16[4,16,1664]{2,1,0:T(8,128)(2,1)S(1)} %pad_maximum_fusion), channel_id=1, source_target_pairs={{0,8},{4,12},{8,0},{12,4},{16,24},{20,28},{24,16},{28,20},{1,9},{5... | collective-permute-start | bytes 638984 | tf_op jit(solution)/shard_map/ppermute | solution.py:41
  26.8 5.4 %collective-permute-start.6 = (bf16[16,16,1664]{2,1,0:T(8,128)(2,1)}, bf16[16,16,1664]{2,1,0:T(8,128)(2,1)S(1)}, u32[]{:S(2)}, u32[]{:S(2)}) collective-permute-start(bf16[16,16,1664]{2,1,0:T(8,128)(2,1)} %get-tuple-element.15), channel_id=1, source_target_pairs={{0,4},{4,0},{8,12},{12,8},{16,20},{20,16},{24,28},{28,24},{1,5},{5... | collective-permute-start | bytes 2555912 | tf_op jit(solution)/shard_map/ppermute | solution.py:41
  27.8 4.6 %collective-permute-start.8 = (bf16[8,16,512]{2,1,0:T(8,128)(2,1)S(1)}, bf16[8,16,512]{2,1,0:T(8,128)(2,1)S(1)}, u32[]{:S(2)}, u32[]{:S(2)}) collective-permute-start(bf16[8,16,512]{2,1,0:T(8,128)(2,1)S(1)} %get-tuple-element.13), channel_id=1, source_target_pairs={{4,0},{8,4},{12,8},{16,12},{20,16},{24,20},{28,24},{5,1},{9,5},{13... | collective-permute-start | bytes 393224 | tf_op jit(solution)/shard_map/ppermute | solution.py:269
  29.1 4.0 %collective-permute-start.7 = (bf16[8,16,512]{2,1,0:T(8,128)(2,1)S(1)}, bf16[8,16,512]{2,1,0:T(8,128)(2,1)S(1)}, u32[]{:S(2)}, u32[]{:S(2)}) collective-permute-start(bf16[8,16,512]{2,1,0:T(8,128)(2,1)S(1)} %get-tuple-element.14), channel_id=1, source_target_pairs={{0,4},{4,8},{8,12},{12,16},{16,20},{20,24},{24,28},{1,5},{5,9},{9,... | collective-permute-start | bytes 393224 | tf_op jit(solution)/shard_map/ppermute | solution.py:268
  32.3 1.2 %copy-start.1 = (bf16[32,16,1664]{2,1,0:T(8,128)(2,1)}, bf16[32,16,1664]{2,1,0:T(8,128)(2,1)S(1)}, u32[]{:S(2)}) copy-start(bf16[32,16,1664]{2,1,0:T(8,128)(2,1)S(1)} %constant_dynamic-update-slice_fusion.7.flat_ref) | copy-start | bytes 5111812
  33.5 3.4 %copy-start = (bf16[8,1024,512]{2,1,0:T(8,128)(2,1)S(1)}, bf16[8,1024,512]{2,1,0:T(8,128)(2,1)}, u32[]{:S(2)}) copy-start(bf16[8,1024,512]{2,1,0:T(8,128)(2,1)} %x_ref.3) | copy-start | bytes 25165828

commit v3 on v2

--- a/solution.py
+++ b/solution.py
@@ -31,16 +31,18 @@
     return stages
 
 
-def gather_relative(block, stages):
-    blocks = block[None]
-    for axis, shift, bits in stages:
+def gather_relative(block, stages, keep):
+    lists = [block[None]]
+    for index, (axis, shift, bits) in enumerate(stages):
+        if index <= len(stages) - keep:
+            lists = [lists[0] if len(lists) == 1 else jnp.concatenate(lists, axis=0)]
         size = lax.axis_size(axis)
-        parts = [blocks]
+        parts = list(lists)
         for m in range(1, 1 << bits):
             pairs = [(i, i ^ (m << shift)) for i in range(size)]
-            parts.append(lax.ppermute(blocks, axis, pairs))
-        blocks = jnp.concatenate(parts, axis=0)
-    return blocks
+            parts += [lax.ppermute(a, axis, pairs) for a in lists]
+        lists = parts
+    return lists
 
 
 def relative_place(seq_xor, batch_xor, stages):
@@ -82,32 +84,44 @@
     o_ref[:, small + LANES :] = w_out[...]
 
 
-def front_kernel(taps, stages, seq_size, batch_size, where_ref, flat_ref, x_ref, left_ref, right_ref,
-                 y_ref, st_ref, wo_ref, pt_ref,
-                 w_scr, wt_scr, bb_scr, p_scr, g_scr, y_scr, s_scr, q_scr):
+def front_kernel(taps, stages, seq_size, batch_size, where_ref, *refs):
+    flat_refs, refs = refs[:-17], refs[-17:]
+    front_body(taps, stages, seq_size, batch_size, where_ref, flat_refs, *refs)
+
+
+def front_body(taps, stages, seq_size, batch_size, where_ref, flat_refs, x_hbm, left_ref, right_ref,
+                 y_ref, st_ref, wo_ref, pt_ref, x_ref,
+                 w_scr, wt_scr, bb_scr, p_scr, g_scr, y_scr, s_scr, q_scr, sems):
     seqs, frames, width = x_ref.shape
     blocks = frames // LANES
-    chunk = y_scr.shape[0] // (seqs * blocks)
+    chunk = y_scr.shape[0] // (seqs * blocks) - 1
     small = 2 * width
     rows = width // (seq_size * batch_size)
     seq_me, batch_me = where_ref[0], where_ref[1]
     first_edge, last_edge = where_ref[2], where_ref[3]
 
+    loads = [pltpu.make_async_copy(x_hbm.at[s], x_ref.at[s], sems.at[s]) for s in range(seqs)]
+    for load in loads:
+        load.start()
+
     for s in range(seq_size):
         for b in range(batch_size):
-            lo = (s * batch_size + b) * rows
-            at = relative_place(seq_me ^ s, batch_me ^ b, stages)
-            w_scr[lo : lo + rows, :] = flat_ref[at, :, 0:small].astype(F32) * 0.5
-            wo_ref[lo : lo + rows, :] = flat_ref[at, :, small + LANES :]
+            at = relative_place(s, b, stages)
+            flat_ref, at = flat_refs[at // flat_refs[0].shape[0]], at % flat_refs[0].shape[0]
+            lo = pl.multiple_of(((seq_me ^ s) * batch_size + (batch_me ^ b)) * rows, rows)
+            w_scr[pl.ds(lo, rows), :] = flat_ref[at, :, 0:small].astype(F32) * 0.5
+            wo_ref[pl.ds(lo, rows), :] = flat_ref[at, :, small + LANES :]
             cell = flat_ref[at, :, small : small + LANES].astype(F32)
             cell = cell + pltpu.roll(cell, LANES // 2, 1)
-            p_scr[lo : lo + rows, :] = cell
+            p_scr[pl.ds(lo, rows), :] = cell
             for h in range(2):
                 col = cell[:, C_B_IN + h : C_B_IN + h + 1] * 0.5
-                bb_scr[2 * lo + h * rows : 2 * lo + (h + 1) * rows, :] = jnp.broadcast_to(col, (rows, LANES))
+                bb_scr[pl.ds(pl.multiple_of(2 * lo + h * rows, rows), rows), :] = jnp.broadcast_to(col, (rows, LANES))
     for j in range(0, small, 256):
         wt_scr[j : j + 256, :] = w_scr[:, j : j + 256].T.astype(BF16)
     pt_ref[...] = p_scr[...].T
+    for load in loads:
+        load.wait()
 
     gain = pt_ref[C_LN_GAIN : C_LN_GAIN + 1, :]
     bias = pt_ref[C_LN_BIAS : C_LN_BIAS + 1, :]
@@ -181,12 +195,12 @@
         zero = jnp.zeros((LANES - reach * SUB, LANES), F32)
         band = jnp.concatenate(low + high + [zero], axis=0).astype(BF16)
         y = jnp.dot(pair, band, preferred_element_type=F32)
-        y_scr[pl.ds(local, seqs * blocks, stride=chunk), :] = y
+        y_scr[pl.ds(local, seqs * blocks, stride=chunk + 1), :] = y
         parts = y.reshape(blocks, seqs, LANES)
         s_scr[pl.ds(c, 1), :] = jnp.sum(jnp.sum(parts, axis=0), axis=0, keepdims=True)
         q_scr[pl.ds(c, 1), :] = jnp.sum(jnp.sum(parts * parts, axis=0), axis=0, keepdims=True)
 
-    unroll = 16
+    unroll = 32
 
     @pl.loop(0, width // chunk)
     def _(n):
@@ -198,17 +212,18 @@
                 local = i * unroll + u
                 channel(base + local, local)
 
-        y_ref[:, pl.ds(base, chunk), :] = y_scr[...].reshape(seqs * blocks, chunk, LANES).astype(BF16)
+        for r in range(seqs * blocks):
+            lo = r * (chunk + 1)
+            y_ref[r, pl.ds(base, chunk), :] = y_scr[lo : lo + chunk, :].astype(BF16)
 
     total = jnp.sum(s_scr[...].T, axis=0, keepdims=True)
     square = jnp.sum(q_scr[...].T, axis=0, keepdims=True)
     st_ref[...] = jnp.broadcast_to(jnp.concatenate([total, square], axis=0)[None], st_ref.shape)
 
 
-def back_kernel(count, st_ref, pt_ref, y_ref, x_ref, wo_ref, o_hbm, scale_scr, shift_scr, o_scr, sems):
+def back_kernel(count, group, st_ref, pt_ref, y_ref, x_ref, wo_ref, o_hbm, scale_scr, shift_scr, o_scr, sems):
     seqs, frames, width = x_ref.shape
     blocks = frames // LANES
-    group = o_scr.shape[1]
     per = seqs // group
     both = jnp.sum(st_ref[...], axis=0)
     mean = both[0:1] * (1.0 / count)
@@ -219,32 +234,36 @@
     shift_scr[...] = jnp.broadcast_to(shift * 0.5, (LANES, width)).T
     out_bias = pt_ref[C_B_OUT : C_B_OUT + 1, :]
 
-    def copy(b, p):
-        target = o_hbm.at[pl.ds(p * group, group), pl.ds(pl.multiple_of(b * LANES, LANES), LANES), :]
-        return pltpu.make_async_copy(o_scr.at[p], target, sems.at[p])
+    def copy(b, s):
+        target = o_hbm.at[s, pl.ds(pl.multiple_of(b * LANES, LANES), LANES), :]
+        slot = lax.rem(b, 2)
+        return pltpu.make_async_copy(o_scr.at[slot, s], target, sems.at[slot, s])
 
     @pl.loop(0, blocks)
     def _(b):
         for p in range(per):
             acts = []
-            for s in range(group):
-                half = y_ref[b * seqs + p * group + s].astype(F32) * scale_scr[...] + shift_scr[...]
+            for s in range(p * group, (p + 1) * group):
+                half = y_ref[b * seqs + s].astype(F32) * scale_scr[...] + shift_scr[...]
                 acts.append((half + half * jnp.tanh(half)).astype(BF16))
             act = jnp.concatenate(acts, axis=1)
             proj = lax.dot_general(act, wo_ref[...], (((0,), (0,)), ((), ())), preferred_element_type=F32)
 
-            @pl.when(b > 0)
+            @pl.when(b > 1)
             def _():
-                copy(b - 1, p).wait()
+                for s in range(p * group, (p + 1) * group):
+                    copy(b - 2, s).wait()
 
             at = pl.multiple_of(b * LANES, LANES)
-            for s in range(group):
-                rest = x_ref[p * group + s, pl.ds(at, LANES), :].astype(F32) + out_bias
-                o_scr[p, s] = proj[LANES * s : LANES * (s + 1)] + rest
-            copy(b, p).start()
-
-    for p in range(per):
-        copy(blocks - 1, p).wait()
+            for q in range(group):
+                s = p * group + q
+                rest = x_ref[s, pl.ds(at, LANES), :].astype(F32) + out_bias
+                o_scr[lax.rem(b, 2), s] = proj[LANES * q : LANES * (q + 1)] + rest
+                copy(b, s).start()
+
+    for b in range(max(blocks - 2, 0), blocks):
+        for s in range(seqs):
+            copy(b, s).wait()
 
 
 def shards(inputs, ln_gain, ln_bias, w_in, b_in, w_depth, bn_gain, bn_bias, w_out, b_out):
@@ -267,59 +286,60 @@
     ends = seq_size - 1
     left = lax.ppermute(inputs[:, frames - HALO :], "seq", [(i, i + 1) for i in range(ends)])
     right = lax.ppermute(inputs[:, :HALO], "seq", [(i + 1, i) for i in range(ends)])
-    flat = gather_relative(packed, stages)
+    flat = gather_relative(packed, stages, 2)
 
     pieces, at = (seq_size, batch_size), (seq_me, batch_me)
     if rows % 16:
         order = jnp.stack([relative_place(seq_me ^ (d // batch_size), batch_me ^ (d % batch_size), stages) for d in range(devices)])
-        flat = jnp.take(flat, order, axis=0)
+        flat = jnp.take(jnp.concatenate(flat, axis=0), order, axis=0)
         for start in (2 * width + C_B_IN, 2 * width + LANES // 2 + C_B_IN):
             cut = flat[:, :, start : start + 2].transpose(0, 2, 1).reshape(2, width).T.reshape(devices, rows, 2)
             flat = lax.dynamic_update_slice(flat, cut, (0, 0, start))
-        flat = flat.reshape(1, width, -1)
+        flat = [flat.reshape(1, width, -1)]
         pieces, at, stages = (1, 1), (0 * seq_me, 0 * batch_me), []
     place = jnp.stack([*at, seq_me == 0, seq_me == ends]).astype(jnp.int32)
 
     chunk = 64
-    x = pltpu.with_memory_space_constraint(inputs, pltpu.VMEM)
-    y, st, wo, pt = pl.pallas_call(
+    y, st, wo, pt, x = pl.pallas_call(
         functools.partial(front_kernel, taps, stages, *pieces),
         out_shape=(
             pltpu.VMEM((seqs * blocks, width, LANES), BF16),
             jax.ShapeDtypeStruct((devices, 2, width), F32),
             pltpu.VMEM((width, width), BF16),
             pltpu.VMEM((LANES, width), F32),
+            pltpu.VMEM((seqs, frames, width), BF16),
         ),
-        in_specs=[pl.BlockSpec(memory_space=pltpu.SMEM)] + [vmem] * 4,
-        out_specs=[vmem] * 4,
+        in_specs=[pl.BlockSpec(memory_space=pltpu.SMEM)] + [vmem] * len(flat) + [pl.BlockSpec(memory_space=pl.ANY)] + [vmem] * 2,
+        out_specs=[vmem] * 5,
         scratch_shapes=[
             pltpu.VMEM((width, 2 * width), F32),
             pltpu.VMEM((2 * width, width), BF16),
             pltpu.VMEM((2 * width, LANES), F32),
             pltpu.VMEM((width, LANES), F32),
             pltpu.VMEM(((blocks + 1) * seqs * width, LANES), F32),
-            pltpu.VMEM((seqs * blocks * chunk, LANES), F32),
-            pltpu.VMEM((width, LANES), F32),
-            pltpu.VMEM((width, LANES), F32),
+            pltpu.VMEM((seqs * blocks * (chunk + 1), LANES), F32),
+            pltpu.VMEM((width, LANES), F32),
+            pltpu.VMEM((width, LANES), F32),
+            pltpu.SemaphoreType.DMA((seqs,)),
         ],
         compiler_params=pltpu.CompilerParams(vmem_limit_bytes=FRONT_VMEM),
         name="front",
-    )(place, flat, x, left, right)
+    )(place, *flat, inputs, left, right)
 
     st = lax.all_to_all(st, ("seq", "batch"), 0, 0)
 
-    group = 4
+    group = 8
     y, x, wo, pt = (pltpu.with_memory_space_constraint(a, pltpu.VMEM) for a in (y, x, wo, pt))
     return pl.pallas_call(
-        functools.partial(back_kernel, float(seqs * frames * devices)),
+        functools.partial(back_kernel, float(seqs * frames * devices), group),
         out_shape=jax.ShapeDtypeStruct((seqs, frames, width), F32),
         in_specs=[vmem] * 5,
         out_specs=pl.BlockSpec(memory_space=pl.ANY),
         scratch_shapes=[
             pltpu.VMEM((width, LANES), F32),
             pltpu.VMEM((width, LANES), F32),
-            pltpu.VMEM((seqs // group, group, LANES, width), F32),
-            pltpu.SemaphoreType.DMA((seqs // group,)),
+            pltpu.VMEM((2, seqs, LANES, width), F32),
+            pltpu.SemaphoreType.DMA((2, seqs)),
         ],
         compiler_params=pltpu.CompilerParams(vmem_limit_bytes=BACK_VMEM),
         name="back",

time: 111 us -> 93.4 us (0.84)
  Pallas kernels: 59.7 us -> 49.8 us
  local copies, waits for them, and re-layouts: 10.4 us -> 2.46 us
  blocking collectives: 16.1 us -> 14.8 us
  starting transfers between devices: 13.5 us -> 14.8 us
    unnamed x10, local copies, waits for them, and re-layouts: 8.6 us -> 1.47 us
    pallas_call x1, Pallas kernels: 44 us -> 38.7 us  [shards(): pl.pallas_call(functools.partial(front_kernel, taps, stages, *pieces), ou...]
    pallas_call x1, Pallas kernels: 14 us -> 9.38 us  [shards(): pl.pallas_call(functools.partial(back_kernel, float(seqs * frames * devic...]
    ppermute x7 -> x10, starting transfers between devices: 9.17 us -> 10.8 us  [gather_relative(): parts += [lax.ppermute(a, axis, pairs) for a in lists]]
    all_to_all x1, blocking collectives: 16.1 us -> 14.8 us  [shards(): st = lax.all_to_all(st, ('seq', 'batch'), 0, 0)]
    ppermute x7 -> x10, waiting for transfers between devices: 9.55 us -> 9.42 us  [gather_relative(): parts += [lax.ppermute(a, axis, pairs) for a in lists]]
  transfers between devices with their start and end apart: 9 -> 12, of which waited for: 4 -> 6; matrix products, arithmetic and copies ran while one was open for 5% -> 1% of each run, Pallas kernels for 0% -> 0%
where the time goes in v3:
time: 93.4 us; the launch traced here: 93.1 us
  Pallas kernels  49.8 us (53%)
  starting transfers between devices  14.8 us (16%)
  blocking collectives  14.8 us (16%)
  waiting for transfers between devices  10.3 us (11%)
  local copies, waits for them, and re-layouts  2.46 us (3%)
    pallas_call x1, Pallas kernels, shards(): pl.pallas_call(functools.partial(front_kernel, taps, stages, *pieces), ou...  38.7 us
    all_to_all x1, blocking collectives, shards(): st = lax.all_to_all(st, ('seq', 'batch'), 0, 0)  14.8 us
    ppermute x10, starting transfers between devices, gather_relative(): parts += [lax.ppermute(a, axis, pairs) for a in lists]  10.8 us
    ppermute x10, waiting for transfers between devices, gather_relative(): parts += [lax.ppermute(a, axis, pairs) for a in lists]  9.42 us
    pallas_call x1, Pallas kernels, shards(): pl.pallas_call(functools.partial(back_kernel, float(seqs * frames * devic...  9.38 us
    ppermute x1, starting transfers between devices, shards(): lax.ppermute(inputs[:, frames - HALO:], 'seq', [(i, i + 1) for i in range...  2.71 us
  transfers between devices with their start and end apart: 12, of which 6 were waited for; matrix products, arithmetic and copies ran while one was open for 1% of the time, Pallas kernels for 0%

profile of v3, /device:TPU:0, one launch (start us, length us, event | category | flops | bytes accessed | tf_op | source)
XLA Modules:
  0.0 93.1 jit_solution(15429245088840597904)
XLA Ops:
  0.0 1.7 %pack.1 = bf16[16,1664]{1,0:T(8,128)(2,1)} custom-call(f32[16]{0:T(128)} %ln_gain.1, f32[16]{0:T(128)} %ln_bias.1, bf16[16,1024]{1,0:T(8,128)(2,1)} %w_in.1, f32[32]{0:T(128)} %b_in.1, f32[16,31]{1,0:T(8,128)} %w_depth.1, f32[16]{0:T(128)} %bn_gain.1, f32[16]{0:T(128)} %bn_bias.1, bf16[16,512]{1,0:T(8,128)(2,1)} %w_out.1, f32[16]{0:T(128)} %b_out.1), custom_call_target="tpu_custom_call" | custom-call | tf_op jit(solution)/shard_map/pack/pallas_call | solution.py:279
  1.7 5.0 %collective-permute-start.2 = (bf16[1,16,1664]{2,1,0:T(8,128)(2,1)}, bf16[1,16,1664]{2,1,0:T(8,128)(2,1)S(1)}, u32[]{:S(2)}, u32[]{:S(2)}) collective-permute-start(bf16[1,16,1664]{2,1,0:T(8,128)(2,1)} %bitcast.5), channel_id=1, source_target_pairs={{0,3},{1,2},{2,1},{3,0},{4,7},{5,6},{6,5},{7,4},{8,11},{9,10},{10,... | collective-permute-start | bytes 159752 | tf_op jit(solution)/shard_map/ppermute | solution.py:43
  6.7 0.6 collective-permute-start
  7.3 2.0 %collective-permute-done.2 = bf16[1,16,1664]{2,1,0:T(8,128)(2,1)S(1)} collective-permute-done((bf16[1,16,1664]{2,1,0:T(8,128)(2,1)}, bf16[1,16,1664]{2,1,0:T(8,128)(2,1)S(1)}, u32[]{:S(2)}, u32[]{:S(2)}) %collective-permute-start.2) | collective-permute-done | bytes 53280 | tf_op jit(solution)/shard_map/ppermute | solution.py:43
  9.3 2.7 %collective-permute-done.1 = bf16[1,16,1664]{2,1,0:T(8,128)(2,1)S(1)} collective-permute-done((bf16[1,16,1664]{2,1,0:T(8,128)(2,1)}, bf16[1,16,1664]{2,1,0:T(8,128)(2,1)S(1)}, u32[]{:S(2)}, u32[]{:S(2)}) %collective-permute-start.1) | collective-permute-done | bytes 53280 | tf_op jit(solution)/shard_map/ppermute | solution.py:43
  12.0 0.8 pad_maximum_fusion.refs_0_
  12.8 2.5 %collective-permute-start.5 = (bf16[4,16,1664]{2,1,0:T(8,128)(2,1)S(1)}, bf16[4,16,1664]{2,1,0:T(8,128)(2,1)S(1)}, u32[]{:S(2)}, u32[]{:S(2)}) collective-permute-start(bf16[4,16,1664]{2,1,0:T(8,128)(2,1)S(1)} %pad_maximum_fusion.refs_0_), channel_id=1, source_target_pairs={{0,24},{4,28},{8,16},{12,20},{16,8},{20,12},{24,0},{28,4},{1,25},{... | collective-permute-start | bytes 638984 | tf_op jit(solution)/shard_map/ppermute | solution.py:43
  15.3 0.5 collective-permute-start.4
  15.9 0.5 collective-permute-start.3
  16.4 1.0 %fusion = (bf16[8,16,512]{2,1,0:T(8,128)(2,1)S(1)}, bf16[8,16,512]{2,1,0:T(8,128)(2,1)S(1)}) fusion(bf16[8,1024,512]{2,1,0:T(8,128)(2,1)} %refs_8_.1), kind=kLoop, calls=%fused_computation.2 | loop fusion | bytes 524288 | tf_op jit(solution)/shard_map/slice | solution.py:288
  17.4 1.3 %collective-permute-start.11 = (bf16[8,16,512]{2,1,0:T(8,128)(2,1)S(1)}, bf16[8,16,512]{2,1,0:T(8,128)(2,1)S(1)}, u32[]{:S(2)}, u32[]{:S(2)}) collective-permute-start(bf16[8,16,512]{2,1,0:T(8,128)(2,1)S(1)} %get-tuple-element.15), channel_id=1, source_target_pairs={{4,0},{8,4},{12,8},{16,12},{20,16},{24,20},{28,24},{5,1},{9,5},{13... | collective-permute-start | bytes 393224 | tf_op jit(solution)/shard_map/ppermute | solution.py:288
  18.7 1.2 %collective-permute-start.6 = (bf16[4,16,1664]{2,1,0:T(8,128)(2,1)S(1)}, bf16[4,16,1664]{2,1,0:T(8,128)(2,1)S(1)}, u32[]{:S(2)}, u32[]{:S(2)}) collective-permute-start(bf16[4,16,1664]{2,1,0:T(8,128)(2,1)S(1)} %pad_maximum_fusion.refs_0_), channel_id=1, source_target_pairs={{0,4},{4,0},{8,12},{12,8},{16,20},{20,16},{24,28},{28,24},{1,5},{5... | collective-permute-start | bytes 638984 | tf_op jit(solution)/shard_map/ppermute | solution.py:43
  19.9 2.1 %collective-permute-done.5.refs_3_ = bf16[4,16,1664]{2,1,0:T(8,128)(2,1)S(1)} collective-permute-done((bf16[4,16,1664]{2,1,0:T(8,128)(2,1)S(1)}, bf16[4,16,1664]{2,1,0:T(8,128)(2,1)S(1)}, u32[]{:S(2)}, u32[]{:S(2)}) %collective-permute-start.5) | collective-permute-done | bytes 213024 | tf_op jit(solution)/shard_map/ppermute | solution.py:43
  22.0 2.5 %collective-permute-done.4.refs_2_ = bf16[4,16,1664]{2,1,0:T(8,128)(2,1)S(1)} collective-permute-done((bf16[4,16,1664]{2,1,0:T(8,128)(2,1)S(1)}, bf16[4,16,1664]{2,1,0:T(8,128)(2,1)S(1)}, u32[]{:S(2)}, u32[]{:S(2)}) %collective-permute-start.4) | collective-permute-done | bytes 213024 | tf_op jit(solution)/shard_map/ppermute | solution.py:43
  24.5 0.1 collective-permute-done.3.refs_1_
  24.6 0.4 collective-permute-start.7
  25.0 2.7 %collective-permute-start.10 = (bf16[8,16,512]{2,1,0:T(8,128)(2,1)S(1)}, bf16[8,16,512]{2,1,0:T(8,128)(2,1)S(1)}, u32[]{:S(2)}, u32[]{:S(2)}) collective-permute-start(bf16[8,16,512]{2,1,0:T(8,128)(2,1)S(1)} %get-tuple-element.16), channel_id=1, source_target_pairs={{0,4},{4,8},{8,12},{12,16},{16,20},{20,24},{24,28},{1,5},{5,9},{9,... | collective-permute-start | bytes 393224 | tf_op jit(solution)/shard_map/ppermute | solution.py:287
  27.8 0.1 pad_add_fusion.where_ref
  27.8 0.9 collective-permute-done.10.refs_9_
  28.8 0.6 copy-done.1
  29.5 0.7 copy-done.4
  30.2 38.7 %front.1 = (bf16[64,512,128]{2,1,0:T(8,128)(2,1)S(1)}, f32[32,2,512]{2,1,0:T(2,128)S(1)}, bf16[512,512]{1,0:T(8,128)(2,1)S(1)}, f32[128,512]{1,0:T(8,128)S(1)}, bf16[8,1024,512]{2,1,0:T(8,128)(2,1)S(1)}) custom-call(s32[4]{0:T(128)S(1)} %pad_add_fusion.where_ref, bf16[4,16,1664]{2,1,0:T(8,128)(2,1)S(1)} %pad_maximum_fusion.refs_0_, ...), custom_call_target="tpu_custom_call" | custom-call | tf_op jit(solution)/shard_map/front/pallas_call | solution.py:303
  69.0 14.8 %all_to_all.5.st_ref = f32[32,2,512]{2,1,0:T(2,128)S(1)} all-to-all(f32[32,2,512]{2,1,0:T(2,128)S(1)} %get-tuple-element.10), channel_id=1, replica_groups=mesh['seq'=8,'batch'=4] {'seq','batch'}, dimensions={0} | all-to-all | bytes 262144 | tf_op jit(solution)/shard_map/all_to_all | solution.py:329
  83.7 9.4 %back.1 = f32[8,1024,512]{2,1,0:T(8,128)} custom-call(f32[32,2,512]{2,1,0:T(2,128)S(1)} %all_to_all.5.st_ref, f32[128,512]{1,0:T(8,128)S(1)} %get-tuple-element.11.pt_ref, bf16[64,512,128]{2,1,0:T(8,128)(2,1)S(1)} %get-tuple-element.12.y_ref, bf16[8,1024,512]{2,1,0:T(8,128)(2,1)S(1)} %get-tuple-element.13.x_ref, bf16[512,512]{1,0:T(8,128)(2,1)S(1)} %get-tuple-element.14.wo_ref), custom_call_target="tpu_custom_call" | custom-call | tf_op jit(solution)/shard_map/back/pallas_call | solution.py:333
  (17 shorter events, 0.2 us)
Async XLA Ops:
  1.7 7.6 %collective-permute-start.2 = (bf16[1,16,1664]{2,1,0:T(8,128)(2,1)}, bf16[1,16,1664]{2,1,0:T(8,128)(2,1)S(1)}, u32[]{:S(2)}, u32[]{:S(2)}) collective-permute-start(bf16[1,16,1664]{2,1,0:T(8,128)(2,1)} %bitcast.5), channel_id=1, source_target_pairs={{0,3},{1,2},{2,1},{3,0},{4,7},{5,6},{6,5},{7,4},{8,11},{9,10},{10,... | collective-permute-start | bytes 159752 | tf_op jit(solution)/shard_map/ppermute | solution.py:43
  6.7 5.2 %collective-permute-start.1 = (bf16[1,16,1664]{2,1,0:T(8,128)(2,1)}, bf16[1,16,1664]{2,1,0:T(8,128)(2,1)S(1)}, u32[]{:S(2)}, u32[]{:S(2)}) collective-permute-start(bf16[1,16,1664]{2,1,0:T(8,128)(2,1)} %bitcast.6), channel_id=1, source_target_pairs={{0,2},{1,3},{2,0},{3,1},{4,6},{5,7},{6,4},{7,5},{8,10},{9,11},{10,... | collective-permute-start | bytes 159752 | tf_op jit(solution)/shard_map/ppermute | solution.py:43
  6.7 5.2 %collective-permute-start = (bf16[1,16,1664]{2,1,0:T(8,128)(2,1)}, bf16[1,16,1664]{2,1,0:T(8,128)(2,1)S(1)}, u32[]{:S(2)}, u32[]{:S(2)}) collective-permute-start(bf16[1,16,1664]{2,1,0:T(8,128)(2,1)} %bitcast.7), channel_id=1, source_target_pairs={{0,1},{1,0},{2,3},{3,2},{4,5},{5,4},{6,7},{7,6},{8,9},{9,8},{10,11... | collective-permute-start | bytes 159752 | tf_op jit(solution)/shard_map/ppermute | solution.py:43
  12.8 9.2 %collective-permute-start.5 = (bf16[4,16,1664]{2,1,0:T(8,128)(2,1)S(1)}, bf16[4,16,1664]{2,1,0:T(8,128)(2,1)S(1)}, u32[]{:S(2)}, u32[]{:S(2)}) collective-permute-start(bf16[4,16,1664]{2,1,0:T(8,128)(2,1)S(1)} %pad_maximum_fusion.refs_0_), channel_id=1, source_target_pairs={{0,24},{4,28},{8,16},{12,20},{16,8},{20,12},{24,0},{28,4},{1,25},{... | collective-permute-start | bytes 638984 | tf_op jit(solution)/shard_map/ppermute | solution.py:43
  15.3 9.2 %collective-permute-start.4 = (bf16[4,16,1664]{2,1,0:T(8,128)(2,1)S(1)}, bf16[4,16,1664]{2,1,0:T(8,128)(2,1)S(1)}, u32[]{:S(2)}, u32[]{:S(2)}) collective-permute-start(bf16[4,16,1664]{2,1,0:T(8,128)(2,1)S(1)} %pad_maximum_fusion.refs_0_), channel_id=1, source_target_pairs={{0,16},{4,20},{8,24},{12,28},{16,0},{20,4},{24,8},{28,12},{1,17},{... | collective-permute-start | bytes 638984 | tf_op jit(solution)/shard_map/ppermute | solution.py:43
  15.9 8.8 %collective-permute-start.3 = (bf16[4,16,1664]{2,1,0:T(8,128)(2,1)S(1)}, bf16[4,16,1664]{2,1,0:T(8,128)(2,1)S(1)}, u32[]{:S(2)}, u32[]{:S(2)}) collective-permute-start(bf16[4,16,1664]{2,1,0:T(8,128)(2,1)S(1)} %pad_maximum_fusion.refs_0_), channel_id=1, source_target_pairs={{0,8},{4,12},{8,0},{12,4},{16,24},{20,28},{24,16},{28,20},{1,9},{5... | collective-permute-start | bytes 638984 | tf_op jit(solution)/shard_map/ppermute | solution.py:43
  17.4 7.7 %collective-permute-start.11 = (bf16[8,16,512]{2,1,0:T(8,128)(2,1)S(1)}, bf16[8,16,512]{2,1,0:T(8,128)(2,1)S(1)}, u32[]{:S(2)}, u32[]{:S(2)}) collective-permute-start(bf16[8,16,512]{2,1,0:T(8,128)(2,1)S(1)} %get-tuple-element.15), channel_id=1, source_target_pairs={{4,0},{8,4},{12,8},{16,12},{20,16},{24,20},{28,24},{5,1},{9,5},{13... | collective-permute-start | bytes 393224 | tf_op jit(solution)/shard_map/ppermute | solution.py:288
  18.7 10.0 %collective-permute-start.6 = (bf16[4,16,1664]{2,1,0:T(8,128)(2,1)S(1)}, bf16[4,16,1664]{2,1,0:T(8,128)(2,1)S(1)}, u32[]{:S(2)}, u32[]{:S(2)}) collective-permute-start(bf16[4,16,1664]{2,1,0:T(8,128)(2,1)S(1)} %pad_maximum_fusion.refs_0_), channel_id=1, source_target_pairs={{0,4},{4,0},{8,12},{12,8},{16,20},{20,16},{24,28},{28,24},{1,5},{5... | collective-permute-start | bytes 638984 | tf_op jit(solution)/shard_map/ppermute | solution.py:43
  22.0 6.8 %copy-start = (bf16[4,16,1664]{2,1,0:T(8,128)(2,1)}, bf16[4,16,1664]{2,1,0:T(8,128)(2,1)S(1)}, u32[]{:S(2)}) copy-start(bf16[4,16,1664]{2,1,0:T(8,128)(2,1)S(1)} %collective-permute-done.5.refs_3_) | copy-start | bytes 638980
  22.0 6.7 %collective-permute-start.9 = (bf16[4,16,1664]{2,1,0:T(8,128)(2,1)S(1)}, bf16[4,16,1664]{2,1,0:T(8,128)(2,1)S(1)}, u32[]{:S(2)}, u32[]{:S(2)}) collective-permute-start(bf16[4,16,1664]{2,1,0:T(8,128)(2,1)S(1)} %collective-permute-done.5.refs_3_), channel_id=1, source_target_pairs={{0,4},{4,0},{8,12},{12,8},{16,20},{20,16},{24,28},{28,24},{1,5},{5... | collective-permute-start | bytes 638984 | tf_op jit(solution)/shard_map/ppermute | solution.py:43
  24.5 4.2 %collective-permute-start.8 = (bf16[4,16,1664]{2,1,0:T(8,128)(2,1)S(1)}, bf16[4,16,1664]{2,1,0:T(8,128)(2,1)S(1)}, u32[]{:S(2)}, u32[]{:S(2)}) collective-permute-start(bf16[4,16,1664]{2,1,0:T(8,128)(2,1)S(1)} %collective-permute-done.4.refs_2_), channel_id=1, source_target_pairs={{0,4},{4,0},{8,12},{12,8},{16,20},{20,16},{24,28},{28,24},{1,5},{5... | collective-permute-start | bytes 638984 | tf_op jit(solution)/shard_map/ppermute | solution.py:43
  24.6 4.1 %collective-permute-start.7 = (bf16[4,16,1664]{2,1,0:T(8,128)(2,1)S(1)}, bf16[4,16,1664]{2,1,0:T(8,128)(2,1)S(1)}, u32[]{:S(2)}, u32[]{:S(2)}) collective-permute-start(bf16[4,16,1664]{2,1,0:T(8,128)(2,1)S(1)} %collective-permute-done.3.refs_1_), channel_id=1, source_target_pairs={{0,4},{4,0},{8,12},{12,8},{16,20},{20,16},{24,28},{28,24},{1,5},{5... | collective-permute-start | bytes 638984 | tf_op jit(solution)/shard_map/ppermute | solution.py:43
  25.0 3.7 %collective-permute-start.10 = (bf16[8,16,512]{2,1,0:T(8,128)(2,1)S(1)}, bf16[8,16,512]{2,1,0:T(8,128)(2,1)S(1)}, u32[]{:S(2)}, u32[]{:S(2)}) collective-permute-start(bf16[8,16,512]{2,1,0:T(8,128)(2,1)S(1)} %get-tuple-element.16), channel_id=1, source_target_pairs={{0,4},{4,8},{8,12},{12,16},{16,20},{20,24},{24,28},{1,5},{5,9},{9,... | collective-permute-start | bytes 393224 | tf_op jit(solution)/shard_map/ppermute | solution.py:287
  28.7 0.7 copy-start.1
  28.7 0.7 copy-start.2
  28.7 0.8 copy-start.3
  29.5 0.7 copy-start.4

commit v4 on v3

--- a/solution.py
+++ b/solution.py
@@ -149,8 +149,9 @@
                 part = glu[:, h * LANES : (h + 1) * LANES]
                 if edge is not None:
                     part = jnp.where(lane >= edge, part, 0.0)
-                to = (b * seqs + s + h) * width
-                g_scr[pl.ds(to if isinstance(b, int) else pl.multiple_of(to, width), width), :] = part
+                to = b * seqs * (width + 1)
+                to = to if isinstance(b, int) else pl.multiple_of(to, SUB)
+                g_scr[pl.ds(to + (s + h) * (width + 1), width), :] = part
 
     block(0, lambda s: jnp.concatenate([left_ref[s], x_ref[s, : LANES - HALO, :]], axis=0), HALO * first_edge)
 
@@ -170,7 +171,7 @@
         move = (s % per) * tail
         if move:
             part = pltpu.roll(part, LANES - move, 1)
-        to = (blocks * seqs + s) * width
+        to = (blocks * seqs + s) * (width + 1)
         g_scr[to : to + width, :] = jnp.where(lane < tail - HALO * last_edge, part, 0.0)
 
     wide = lax.broadcasted_iota(jnp.int32, (SUB, LANES), 1)
@@ -178,7 +179,7 @@
     reach = 4
 
     def channel(c, local):
-        g = g_scr[pl.ds(c, seqs * (blocks + 1), stride=width), :]
+        g = g_scr[pl.ds(c, seqs * (blocks + 1), stride=width + 1), :]
         pair = jnp.concatenate([g[: seqs * blocks].astype(BF16), g[seqs:].astype(BF16)], axis=1)
         tap = jnp.broadcast_to(p_scr[pl.ds(c, 1), :], (SUB, LANES))
         tap = jnp.where(wide >= LANES - taps, tap, 0.0)
@@ -316,7 +317,7 @@
             pltpu.VMEM((2 * width, width), BF16),
             pltpu.VMEM((2 * width, LANES), F32),
             pltpu.VMEM((width, LANES), F32),
-            pltpu.VMEM(((blocks + 1) * seqs * width, LANES), F32),
+            pltpu.VMEM(((blocks + 1) * seqs * (width + 1), LANES), F32),
             pltpu.VMEM((seqs * blocks * (chunk + 1), LANES), F32),
             pltpu.VMEM((width, LANES), F32),
             pltpu.VMEM((width, LANES), F32),

time: 93.4 us -> 92.5 us (level)
  no operation moved by 1% of the time
where the time goes in v4:
time: 92.5 us; the launch traced here: 92.2 us
  Pallas kernels  48.9 us (53%)
  starting transfers between devices  14.8 us (16%)
  blocking collectives  14.7 us (16%)
  waiting for transfers between devices  10.3 us (11%)
  local copies, waits for them, and re-layouts  2.46 us (3%)
    pallas_call x1, Pallas kernels, shards(): pl.pallas_call(functools.partial(front_kernel, taps, stages, *pieces), ou...  37.9 us
    all_to_all x1, blocking collectives, shards(): st = lax.all_to_all(st, ('seq', 'batch'), 0, 0)  14.7 us
    ppermute x10, starting transfers between devices, gather_relative(): parts += [lax.ppermute(a, axis, pairs) for a in lists]  10.8 us
    ppermute x10, waiting for transfers between devices, gather_relative(): parts += [lax.ppermute(a, axis, pairs) for a in lists]  9.42 us
    pallas_call x1, Pallas kernels, shards(): pl.pallas_call(functools.partial(back_kernel, float(seqs * frames * devic...  9.38 us
    ppermute x1, starting transfers between devices, shards(): lax.ppermute(inputs[:, frames - HALO:], 'seq', [(i, i + 1) for i in range...  2.71 us
  transfers between devices with their start and end apart: 12, of which 6 were waited for; matrix products, arithmetic and copies ran while one was open for 1% of the time, Pallas kernels for 0%

profile of v4, /device:TPU:0, one launch (start us, length us, event | category | flops | bytes accessed | tf_op | source)
XLA Modules:
  0.0 92.2 jit_solution(13416623003126232230)
XLA Ops:
  0.0 1.7 %pack.1 = bf16[16,1664]{1,0:T(8,128)(2,1)} custom-call(f32[16]{0:T(128)} %ln_gain.1, f32[16]{0:T(128)} %ln_bias.1, bf16[16,1024]{1,0:T(8,128)(2,1)} %w_in.1, f32[32]{0:T(128)} %b_in.1, f32[16,31]{1,0:T(8,128)} %w_depth.1, f32[16]{0:T(128)} %bn_gain.1, f32[16]{0:T(128)} %bn_bias.1, bf16[16,512]{1,0:T(8,128)(2,1)} %w_out.1, f32[16]{0:T(128)} %b_out.1), custom_call_target="tpu_custom_call" | custom-call | tf_op jit(solution)/shard_map/pack/pallas_call | solution.py:280
  1.7 5.0 %collective-permute-start.2 = (bf16[1,16,1664]{2,1,0:T(8,128)(2,1)}, bf16[1,16,1664]{2,1,0:T(8,128)(2,1)S(1)}, u32[]{:S(2)}, u32[]{:S(2)}) collective-permute-start(bf16[1,16,1664]{2,1,0:T(8,128)(2,1)} %bitcast.5), channel_id=1, source_target_pairs={{0,3},{1,2},{2,1},{3,0},{4,7},{5,6},{6,5},{7,4},{8,11},{9,10},{10,... | collective-permute-start | bytes 159752 | tf_op jit(solution)/shard_map/ppermute | solution.py:43
  6.7 0.6 collective-permute-start
  7.3 2.0 %collective-permute-done.2 = bf16[1,16,1664]{2,1,0:T(8,128)(2,1)S(1)} collective-permute-done((bf16[1,16,1664]{2,1,0:T(8,128)(2,1)}, bf16[1,16,1664]{2,1,0:T(8,128)(2,1)S(1)}, u32[]{:S(2)}, u32[]{:S(2)}) %collective-permute-start.2) | collective-permute-done | bytes 53280 | tf_op jit(solution)/shard_map/ppermute | solution.py:43
  9.3 2.7 %collective-permute-done.1 = bf16[1,16,1664]{2,1,0:T(8,128)(2,1)S(1)} collective-permute-done((bf16[1,16,1664]{2,1,0:T(8,128)(2,1)}, bf16[1,16,1664]{2,1,0:T(8,128)(2,1)S(1)}, u32[]{:S(2)}, u32[]{:S(2)}) %collective-permute-start.1) | collective-permute-done | bytes 53280 | tf_op jit(solution)/shard_map/ppermute | solution.py:43
  12.0 0.8 pad_maximum_fusion.refs_0_
  12.8 2.5 %collective-permute-start.5 = (bf16[4,16,1664]{2,1,0:T(8,128)(2,1)S(1)}, bf16[4,16,1664]{2,1,0:T(8,128)(2,1)S(1)}, u32[]{:S(2)}, u32[]{:S(2)}) collective-permute-start(bf16[4,16,1664]{2,1,0:T(8,128)(2,1)S(1)} %pad_maximum_fusion.refs_0_), channel_id=1, source_target_pairs={{0,24},{4,28},{8,16},{12,20},{16,8},{20,12},{24,0},{28,4},{1,25},{... | collective-permute-start | bytes 638984 | tf_op jit(solution)/shard_map/ppermute | solution.py:43
  15.3 0.5 collective-permute-start.4
  15.9 0.5 collective-permute-start.3
  16.4 1.0 %fusion = (bf16[8,16,512]{2,1,0:T(8,128)(2,1)S(1)}, bf16[8,16,512]{2,1,0:T(8,128)(2,1)S(1)}) fusion(bf16[8,1024,512]{2,1,0:T(8,128)(2,1)} %refs_8_.1), kind=kLoop, calls=%fused_computation.2 | loop fusion | bytes 524288 | tf_op jit(solution)/shard_map/slice | solution.py:289
  17.4 1.3 %collective-permute-start.11 = (bf16[8,16,512]{2,1,0:T(8,128)(2,1)S(1)}, bf16[8,16,512]{2,1,0:T(8,128)(2,1)S(1)}, u32[]{:S(2)}, u32[]{:S(2)}) collective-permute-start(bf16[8,16,512]{2,1,0:T(8,128)(2,1)S(1)} %get-tuple-element.15), channel_id=1, source_target_pairs={{4,0},{8,4},{12,8},{16,12},{20,16},{24,20},{28,24},{5,1},{9,5},{13... | collective-permute-start | bytes 393224 | tf_op jit(solution)/shard_map/ppermute | solution.py:289
  18.7 1.2 %collective-permute-start.6 = (bf16[4,16,1664]{2,1,0:T(8,128)(2,1)S(1)}, bf16[4,16,1664]{2,1,0:T(8,128)(2,1)S(1)}, u32[]{:S(2)}, u32[]{:S(2)}) collective-permute-start(bf16[4,16,1664]{2,1,0:T(8,128)(2,1)S(1)} %pad_maximum_fusion.refs_0_), channel_id=1, source_target_pairs={{0,4},{4,0},{8,12},{12,8},{16,20},{20,16},{24,28},{28,24},{1,5},{5... | collective-permute-start | bytes 638984 | tf_op jit(solution)/shard_map/ppermute | solution.py:43
  19.9 2.1 %collective-permute-done.5.refs_3_ = bf16[4,16,1664]{2,1,0:T(8,128)(2,1)S(1)} collective-permute-done((bf16[4,16,1664]{2,1,0:T(8,128)(2,1)S(1)}, bf16[4,16,1664]{2,1,0:T(8,128)(2,1)S(1)}, u32[]{:S(2)}, u32[]{:S(2)}) %collective-permute-start.5) | collective-permute-done | bytes 213024 | tf_op jit(solution)/shard_map/ppermute | solution.py:43
  22.0 2.5 %collective-permute-done.4.refs_2_ = bf16[4,16,1664]{2,1,0:T(8,128)(2,1)S(1)} collective-permute-done((bf16[4,16,1664]{2,1,0:T(8,128)(2,1)S(1)}, bf16[4,16,1664]{2,1,0:T(8,128)(2,1)S(1)}, u32[]{:S(2)}, u32[]{:S(2)}) %collective-permute-start.4) | collective-permute-done | bytes 213024 | tf_op jit(solution)/shard_map/ppermute | solution.py:43
  24.5 0.1 collective-permute-done.3.refs_1_
  24.6 0.4 collective-permute-start.7
  25.0 2.7 %collective-permute-start.10 = (bf16[8,16,512]{2,1,0:T(8,128)(2,1)S(1)}, bf16[8,16,512]{2,1,0:T(8,128)(2,1)S(1)}, u32[]{:S(2)}, u32[]{:S(2)}) collective-permute-start(bf16[8,16,512]{2,1,0:T(8,128)(2,1)S(1)} %get-tuple-element.16), channel_id=1, source_target_pairs={{0,4},{4,8},{8,12},{12,16},{16,20},{20,24},{24,28},{1,5},{5,9},{9,... | collective-permute-start | bytes 393224 | tf_op jit(solution)/shard_map/ppermute | solution.py:288
  27.8 0.1 pad_add_fusion.where_ref
  27.8 0.9 collective-permute-done.10.refs_9_
  28.8 0.6 copy-done.1
  29.5 0.7 copy-done.4
  30.2 37.9 %front.1 = (bf16[64,512,128]{2,1,0:T(8,128)(2,1)S(1)}, f32[32,2,512]{2,1,0:T(2,128)S(1)}, bf16[512,512]{1,0:T(8,128)(2,1)S(1)}, f32[128,512]{1,0:T(8,128)S(1)}, bf16[8,1024,512]{2,1,0:T(8,128)(2,1)S(1)}) custom-call(s32[4]{0:T(128)S(1)} %pad_add_fusion.where_ref, bf16[4,16,1664]{2,1,0:T(8,128)(2,1)S(1)} %pad_maximum_fusion.refs_0_, ...), custom_call_target="tpu_custom_call" | custom-call | tf_op jit(solution)/shard_map/front/pallas_call | solution.py:304
  68.1 14.7 %all_to_all.5.st_ref = f32[32,2,512]{2,1,0:T(2,128)S(1)} all-to-all(f32[32,2,512]{2,1,0:T(2,128)S(1)} %get-tuple-element.10), channel_id=1, replica_groups=mesh['seq'=8,'batch'=4] {'seq','batch'}, dimensions={0} | all-to-all | bytes 262144 | tf_op jit(solution)/shard_map/all_to_all | solution.py:330
  82.8 9.4 %back.1 = f32[8,1024,512]{2,1,0:T(8,128)} custom-call(f32[32,2,512]{2,1,0:T(2,128)S(1)} %all_to_all.5.st_ref, f32[128,512]{1,0:T(8,128)S(1)} %get-tuple-element.11.pt_ref, bf16[64,512,128]{2,1,0:T(8,128)(2,1)S(1)} %get-tuple-element.12.y_ref, bf16[8,1024,512]{2,1,0:T(8,128)(2,1)S(1)} %get-tuple-element.13.x_ref, bf16[512,512]{1,0:T(8,128)(2,1)S(1)} %get-tuple-element.14.wo_ref), custom_call_target="tpu_custom_call" | custom-call | tf_op jit(solution)/shard_map/back/pallas_call | solution.py:334
  (17 shorter events, 0.2 us)
Async XLA Ops:
  1.7 7.6 %collective-permute-start.2 = (bf16[1,16,1664]{2,1,0:T(8,128)(2,1)}, bf16[1,16,1664]{2,1,0:T(8,128)(2,1)S(1)}, u32[]{:S(2)}, u32[]{:S(2)}) collective-permute-start(bf16[1,16,1664]{2,1,0:T(8,128)(2,1)} %bitcast.5), channel_id=1, source_target_pairs={{0,3},{1,2},{2,1},{3,0},{4,7},{5,6},{6,5},{7,4},{8,11},{9,10},{10,... | collective-permute-start | bytes 159752 | tf_op jit(solution)/shard_map/ppermute | solution.py:43
  6.7 5.2 %collective-permute-start.1 = (bf16[1,16,1664]{2,1,0:T(8,128)(2,1)}, bf16[1,16,1664]{2,1,0:T(8,128)(2,1)S(1)}, u32[]{:S(2)}, u32[]{:S(2)}) collective-permute-start(bf16[1,16,1664]{2,1,0:T(8,128)(2,1)} %bitcast.6), channel_id=1, source_target_pairs={{0,2},{1,3},{2,0},{3,1},{4,6},{5,7},{6,4},{7,5},{8,10},{9,11},{10,... | collective-permute-start | bytes 159752 | tf_op jit(solution)/shard_map/ppermute | solution.py:43
  6.7 5.2 %collective-permute-start = (bf16[1,16,1664]{2,1,0:T(8,128)(2,1)}, bf16[1,16,1664]{2,1,0:T(8,128)(2,1)S(1)}, u32[]{:S(2)}, u32[]{:S(2)}) collective-permute-start(bf16[1,16,1664]{2,1,0:T(8,128)(2,1)} %bitcast.7), channel_id=1, source_target_pairs={{0,1},{1,0},{2,3},{3,2},{4,5},{5,4},{6,7},{7,6},{8,9},{9,8},{10,11... | collective-permute-start | bytes 159752 | tf_op jit(solution)/shard_map/ppermute | solution.py:43
  12.8 9.2 %collective-permute-start.5 = (bf16[4,16,1664]{2,1,0:T(8,128)(2,1)S(1)}, bf16[4,16,1664]{2,1,0:T(8,128)(2,1)S(1)}, u32[]{:S(2)}, u32[]{:S(2)}) collective-permute-start(bf16[4,16,1664]{2,1,0:T(8,128)(2,1)S(1)} %pad_maximum_fusion.refs_0_), channel_id=1, source_target_pairs={{0,24},{4,28},{8,16},{12,20},{16,8},{20,12},{24,0},{28,4},{1,25},{... | collective-permute-start | bytes 638984 | tf_op jit(solution)/shard_map/ppermute | solution.py:43
  15.3 9.2 %collective-permute-start.4 = (bf16[4,16,1664]{2,1,0:T(8,128)(2,1)S(1)}, bf16[4,16,1664]{2,1,0:T(8,128)(2,1)S(1)}, u32[]{:S(2)}, u32[]{:S(2)}) collective-permute-start(bf16[4,16,1664]{2,1,0:T(8,128)(2,1)S(1)} %pad_maximum_fusion.refs_0_), channel_id=1, source_target_pairs={{0,16},{4,20},{8,24},{12,28},{16,0},{20,4},{24,8},{28,12},{1,17},{... | collective-permute-start | bytes 638984 | tf_op jit(solution)/shard_map/ppermute | solution.py:43
  15.9 8.8 %collective-permute-start.3 = (bf16[4,16,1664]{2,1,0:T(8,128)(2,1)S(1)}, bf16[4,16,1664]{2,1,0:T(8,128)(2,1)S(1)}, u32[]{:S(2)}, u32[]{:S(2)}) collective-permute-start(bf16[4,16,1664]{2,1,0:T(8,128)(2,1)S(1)} %pad_maximum_fusion.refs_0_), channel_id=1, source_target_pairs={{0,8},{4,12},{8,0},{12,4},{16,24},{20,28},{24,16},{28,20},{1,9},{5... | collective-permute-start | bytes 638984 | tf_op jit(solution)/shard_map/ppermute | solution.py:43
  17.4 7.7 %collective-permute-start.11 = (bf16[8,16,512]{2,1,0:T(8,128)(2,1)S(1)}, bf16[8,16,512]{2,1,0:T(8,128)(2,1)S(1)}, u32[]{:S(2)}, u32[]{:S(2)}) collective-permute-start(bf16[8,16,512]{2,1,0:T(8,128)(2,1)S(1)} %get-tuple-element.15), channel_id=1, source_target_pairs={{4,0},{8,4},{12,8},{16,12},{20,16},{24,20},{28,24},{5,1},{9,5},{13... | collective-permute-start | bytes 393224 | tf_op jit(solution)/shard_map/ppermute | solution.py:289
  18.7 10.0 %collective-permute-start.6 = (bf16[4,16,1664]{2,1,0:T(8,128)(2,1)S(1)}, bf16[4,16,1664]{2,1,0:T(8,128)(2,1)S(1)}, u32[]{:S(2)}, u32[]{:S(2)}) collective-permute-start(bf16[4,16,1664]{2,1,0:T(8,128)(2,1)S(1)} %pad_maximum_fusion.refs_0_), channel_id=1, source_target_pairs={{0,4},{4,0},{8,12},{12,8},{16,20},{20,16},{24,28},{28,24},{1,5},{5... | collective-permute-start | bytes 638984 | tf_op jit(solution)/shard_map/ppermute | solution.py:43
  22.0 6.8 %copy-start = (bf16[4,16,1664]{2,1,0:T(8,128)(2,1)}, bf16[4,16,1664]{2,1,0:T(8,128)(2,1)S(1)}, u32[]{:S(2)}) copy-start(bf16[4,16,1664]{2,1,0:T(8,128)(2,1)S(1)} %collective-permute-done.5.refs_3_) | copy-start | bytes 638980
  22.0 6.7 %collective-permute-start.9 = (bf16[4,16,1664]{2,1,0:T(8,128)(2,1)S(1)}, bf16[4,16,1664]{2,1,0:T(8,128)(2,1)S(1)}, u32[]{:S(2)}, u32[]{:S(2)}) collective-permute-start(bf16[4,16,1664]{2,1,0:T(8,128)(2,1)S(1)} %collective-permute-done.5.refs_3_), channel_id=1, source_target_pairs={{0,4},{4,0},{8,12},{12,8},{16,20},{20,16},{24,28},{28,24},{1,5},{5... | collective-permute-start | bytes 638984 | tf_op jit(solution)/shard_map/ppermute | solution.py:43
  24.5 4.2 %collective-permute-start.8 = (bf16[4,16,1664]{2,1,0:T(8,128)(2,1)S(1)}, bf16[4,16,1664]{2,1,0:T(8,128)(2,1)S(1)}, u32[]{:S(2)}, u32[]{:S(2)}) collective-permute-start(bf16[4,16,1664]{2,1,0:T(8,128)(2,1)S(1)} %collective-permute-done.4.refs_2_), channel_id=1, source_target_pairs={{0,4},{4,0},{8,12},{12,8},{16,20},{20,16},{24,28},{28,24},{1,5},{5... | collective-permute-start | bytes 638984 | tf_op jit(solution)/shard_map/ppermute | solution.py:43
  24.6 4.1 %collective-permute-start.7 = (bf16[4,16,1664]{2,1,0:T(8,128)(2,1)S(1)}, bf16[4,16,1664]{2,1,0:T(8,128)(2,1)S(1)}, u32[]{:S(2)}, u32[]{:S(2)}) collective-permute-start(bf16[4,16,1664]{2,1,0:T(8,128)(2,1)S(1)} %collective-permute-done.3.refs_1_), channel_id=1, source_target_pairs={{0,4},{4,0},{8,12},{12,8},{16,20},{20,16},{24,28},{28,24},{1,5},{5... | collective-permute-start | bytes 638984 | tf_op jit(solution)/shard_map/ppermute | solution.py:43
  25.0 3.7 %collective-permute-start.10 = (bf16[8,16,512]{2,1,0:T(8,128)(2,1)S(1)}, bf16[8,16,512]{2,1,0:T(8,128)(2,1)S(1)}, u32[]{:S(2)}, u32[]{:S(2)}) collective-permute-start(bf16[8,16,512]{2,1,0:T(8,128)(2,1)S(1)} %get-tuple-element.16), channel_id=1, source_target_pairs={{0,4},{4,8},{8,12},{12,16},{16,20},{20,24},{24,28},{1,5},{5,9},{9,... | collective-permute-start | bytes 393224 | tf_op jit(solution)/shard_map/ppermute | solution.py:288
  28.7 0.7 copy-start.1
  28.7 0.7 copy-start.2
  28.7 0.8 copy-start.3
  29.5 0.7 copy-start.4

commit v5 on v4

--- a/solution.py
+++ b/solution.py
@@ -120,8 +120,6 @@
     for j in range(0, small, 256):
         wt_scr[j : j + 256, :] = w_scr[:, j : j + 256].T.astype(BF16)
     pt_ref[...] = p_scr[...].T
-    for load in loads:
-        load.wait()
 
     gain = pt_ref[C_LN_GAIN : C_LN_GAIN + 1, :]
     bias = pt_ref[C_LN_BIAS : C_LN_BIAS + 1, :]
@@ -153,7 +151,11 @@
                 to = to if isinstance(b, int) else pl.multiple_of(to, SUB)
                 g_scr[pl.ds(to + (s + h) * (width + 1), width), :] = part
 
-    block(0, lambda s: jnp.concatenate([left_ref[s], x_ref[s, : LANES - HALO, :]], axis=0), HALO * first_edge)
+    def start_piece(s):
+        loads[s].wait()
+        return jnp.concatenate([left_ref[s], x_ref[s, : LANES - HALO, :]], axis=0)
+
+    block(0, start_piece, HALO * first_edge)
 
     @pl.loop(1, blocks)
     def _(b):
@@ -180,7 +182,7 @@
 
     def channel(c, local):
         g = g_scr[pl.ds(c, seqs * (blocks + 1), stride=width + 1), :]
-        pair = jnp.concatenate([g[: seqs * blocks].astype(BF16), g[seqs:].astype(BF16)], axis=1)
+        pair = jnp.concatenate([g[: seqs * blocks].astype(BF16), g[seqs:, : reach * SUB].astype(BF16)], axis=1)
         tap = jnp.broadcast_to(p_scr[pl.ds(c, 1), :], (SUB, LANES))
         tap = jnp.where(wide >= LANES - taps, tap, 0.0)
         first = pltpu.roll(tap, 0, 1, stride=1, stride_axis=0)
@@ -193,8 +195,7 @@
                 high.append(jnp.where(under, 0.0, f))
             else:
                 low.append(f)
-        zero = jnp.zeros((LANES - reach * SUB, LANES), F32)
-        band = jnp.concatenate(low + high + [zero], axis=0).astype(BF16)
+        band = jnp.concatenate(low + high, axis=0).astype(BF16)
         y = jnp.dot(pair, band, preferred_element_type=F32)
         y_scr[pl.ds(local, seqs * blocks, stride=chunk + 1), :] = y
         parts = y.reshape(blocks, seqs, LANES)

time: 92.5 us -> 92.8 us (level)
  no operation moved by 1% of the time
where the time goes in v5:
time: 92.8 us; the launch traced here: 92.5 us
  Pallas kernels  49.2 us (53%)
  starting transfers between devices  14.8 us (16%)
  blocking collectives  14.7 us (16%)
  waiting for transfers between devices  10.3 us (11%)
  local copies, waits for them, and re-layouts  2.46 us (3%)
    pallas_call x1, Pallas kernels, shards(): pl.pallas_call(functools.partial(front_kernel, taps, stages, *pieces), ou...  38.1 us
    all_to_all x1, blocking collectives, shards(): st = lax.all_to_all(st, ('seq', 'batch'), 0, 0)  14.7 us
    ppermute x10, starting transfers between devices, gather_relative(): parts += [lax.ppermute(a, axis, pairs) for a in lists]  10.8 us
    ppermute x10, waiting for transfers between devices, gather_relative(): parts += [lax.ppermute(a, axis, pairs) for a in lists]  9.42 us
    pallas_call x1, Pallas kernels, shards(): pl.pallas_call(functools.partial(back_kernel, float(seqs * frames * devic...  9.37 us
    ppermute x1, starting transfers between devices, shards(): lax.ppermute(inputs[:, frames - HALO:], 'seq', [(i, i + 1) for i in range...  2.71 us
  transfers between devices with their start and end apart: 12, of which 6 were waited for; matrix products, arithmetic and copies ran while one was open for 1% of the time, Pallas kernels for 0%

profile of v5, /device:TPU:0, one launch (start us, length us, event | category | flops | bytes accessed | tf_op | source)
XLA Modules:
  0.0 92.5 jit_solution(13551023276416927890)
XLA Ops:
  0.0 1.7 %pack.1 = bf16[16,1664]{1,0:T(8,128)(2,1)} custom-call(f32[16]{0:T(128)} %ln_gain.1, f32[16]{0:T(128)} %ln_bias.1, bf16[16,1024]{1,0:T(8,128)(2,1)} %w_in.1, f32[32]{0:T(128)} %b_in.1, f32[16,31]{1,0:T(8,128)} %w_depth.1, f32[16]{0:T(128)} %bn_gain.1, f32[16]{0:T(128)} %bn_bias.1, bf16[16,512]{1,0:T(8,128)(2,1)} %w_out.1, f32[16]{0:T(128)} %b_out.1), custom_call_target="tpu_custom_call" | custom-call | tf_op jit(solution)/shard_map/pack/pallas_call | solution.py:281
  1.7 5.0 %collective-permute-start.2 = (bf16[1,16,1664]{2,1,0:T(8,128)(2,1)}, bf16[1,16,1664]{2,1,0:T(8,128)(2,1)S(1)}, u32[]{:S(2)}, u32[]{:S(2)}) collective-permute-start(bf16[1,16,1664]{2,1,0:T(8,128)(2,1)} %bitcast.5), channel_id=1, source_target_pairs={{0,3},{1,2},{2,1},{3,0},{4,7},{5,6},{6,5},{7,4},{8,11},{9,10},{10,... | collective-permute-start | bytes 159752 | tf_op jit(solution)/shard_map/ppermute | solution.py:43
  6.7 0.6 collective-permute-start
  7.3 2.0 %collective-permute-done.2 = bf16[1,16,1664]{2,1,0:T(8,128)(2,1)S(1)} collective-permute-done((bf16[1,16,1664]{2,1,0:T(8,128)(2,1)}, bf16[1,16,1664]{2,1,0:T(8,128)(2,1)S(1)}, u32[]{:S(2)}, u32[]{:S(2)}) %collective-permute-start.2) | collective-permute-done | bytes 53280 | tf_op jit(solution)/shard_map/ppermute | solution.py:43
  9.3 2.7 %collective-permute-done.1 = bf16[1,16,1664]{2,1,0:T(8,128)(2,1)S(1)} collective-permute-done((bf16[1,16,1664]{2,1,0:T(8,128)(2,1)}, bf16[1,16,1664]{2,1,0:T(8,128)(2,1)S(1)}, u32[]{:S(2)}, u32[]{:S(2)}) %collective-permute-start.1) | collective-permute-done | bytes 53280 | tf_op jit(solution)/shard_map/ppermute | solution.py:43
  12.0 0.8 pad_maximum_fusion.refs_0_
  12.8 2.5 %collective-permute-start.5 = (bf16[4,16,1664]{2,1,0:T(8,128)(2,1)S(1)}, bf16[4,16,1664]{2,1,0:T(8,128)(2,1)S(1)}, u32[]{:S(2)}, u32[]{:S(2)}) collective-permute-start(bf16[4,16,1664]{2,1,0:T(8,128)(2,1)S(1)} %pad_maximum_fusion.refs_0_), channel_id=1, source_target_pairs={{0,24},{4,28},{8,16},{12,20},{16,8},{20,12},{24,0},{28,4},{1,25},{... | collective-permute-start | bytes 638984 | tf_op jit(solution)/shard_map/ppermute | solution.py:43
  15.3 0.5 collective-permute-start.4
  15.9 0.5 collective-permute-start.3
  16.4 1.0 %fusion = (bf16[8,16,512]{2,1,0:T(8,128)(2,1)S(1)}, bf16[8,16,512]{2,1,0:T(8,128)(2,1)S(1)}) fusion(bf16[8,1024,512]{2,1,0:T(8,128)(2,1)} %refs_8_.1), kind=kLoop, calls=%fused_computation.2 | loop fusion | bytes 524288 | tf_op jit(solution)/shard_map/slice | solution.py:290
  17.4 1.3 %collective-permute-start.11 = (bf16[8,16,512]{2,1,0:T(8,128)(2,1)S(1)}, bf16[8,16,512]{2,1,0:T(8,128)(2,1)S(1)}, u32[]{:S(2)}, u32[]{:S(2)}) collective-permute-start(bf16[8,16,512]{2,1,0:T(8,128)(2,1)S(1)} %get-tuple-element.15), channel_id=1, source_target_pairs={{4,0},{8,4},{12,8},{16,12},{20,16},{24,20},{28,24},{5,1},{9,5},{13... | collective-permute-start | bytes 393224 | tf_op jit(solution)/shard_map/ppermute | solution.py:290
  18.7 1.2 %collective-permute-start.6 = (bf16[4,16,1664]{2,1,0:T(8,128)(2,1)S(1)}, bf16[4,16,1664]{2,1,0:T(8,128)(2,1)S(1)}, u32[]{:S(2)}, u32[]{:S(2)}) collective-permute-start(bf16[4,16,1664]{2,1,0:T(8,128)(2,1)S(1)} %pad_maximum_fusion.refs_0_), channel_id=1, source_target_pairs={{0,4},{4,0},{8,12},{12,8},{16,20},{20,16},{24,28},{28,24},{1,5},{5... | collective-permute-start | bytes 638984 | tf_op jit(solution)/shard_map/ppermute | solution.py:43
  19.9 2.1 %collective-permute-done.5.refs_3_ = bf16[4,16,1664]{2,1,0:T(8,128)(2,1)S(1)} collective-permute-done((bf16[4,16,1664]{2,1,0:T(8,128)(2,1)S(1)}, bf16[4,16,1664]{2,1,0:T(8,128)(2,1)S(1)}, u32[]{:S(2)}, u32[]{:S(2)}) %collective-permute-start.5) | collective-permute-done | bytes 213024 | tf_op jit(solution)/shard_map/ppermute | solution.py:43
  22.0 2.5 %collective-permute-done.4.refs_2_ = bf16[4,16,1664]{2,1,0:T(8,128)(2,1)S(1)} collective-permute-done((bf16[4,16,1664]{2,1,0:T(8,128)(2,1)S(1)}, bf16[4,16,1664]{2,1,0:T(8,128)(2,1)S(1)}, u32[]{:S(2)}, u32[]{:S(2)}) %collective-permute-start.4) | collective-permute-done | bytes 213024 | tf_op jit(solution)/shard_map/ppermute | solution.py:43
  24.5 0.1 collective-permute-done.3.refs_1_
  24.6 0.4 collective-permute-start.7
  25.0 2.7 %collective-permute-start.10 = (bf16[8,16,512]{2,1,0:T(8,128)(2,1)S(1)}, bf16[8,16,512]{2,1,0:T(8,128)(2,1)S(1)}, u32[]{:S(2)}, u32[]{:S(2)}) collective-permute-start(bf16[8,16,512]{2,1,0:T(8,128)(2,1)S(1)} %get-tuple-element.16), channel_id=1, source_target_pairs={{0,4},{4,8},{8,12},{12,16},{16,20},{20,24},{24,28},{1,5},{5,9},{9,... | collective-permute-start | bytes 393224 | tf_op jit(solution)/shard_map/ppermute | solution.py:289
  27.8 0.1 pad_add_fusion.where_ref
  27.8 0.9 collective-permute-done.10.refs_9_
  28.8 0.6 copy-done.1
  29.5 0.7 copy-done.4
  30.2 38.1 %front.1 = (bf16[64,512,128]{2,1,0:T(8,128)(2,1)S(1)}, f32[32,2,512]{2,1,0:T(2,128)S(1)}, bf16[512,512]{1,0:T(8,128)(2,1)S(1)}, f32[128,512]{1,0:T(8,128)S(1)}, bf16[8,1024,512]{2,1,0:T(8,128)(2,1)S(1)}) custom-call(s32[4]{0:T(128)S(1)} %pad_add_fusion.where_ref, bf16[4,16,1664]{2,1,0:T(8,128)(2,1)S(1)} %pad_maximum_fusion.refs_0_, ...), custom_call_target="tpu_custom_call" | custom-call | tf_op jit(solution)/shard_map/front/pallas_call | solution.py:305
  68.4 14.7 %all_to_all.5.st_ref = f32[32,2,512]{2,1,0:T(2,128)S(1)} all-to-all(f32[32,2,512]{2,1,0:T(2,128)S(1)} %get-tuple-element.10), channel_id=1, replica_groups=mesh['seq'=8,'batch'=4] {'seq','batch'}, dimensions={0} | all-to-all | bytes 262144 | tf_op jit(solution)/shard_map/all_to_all | solution.py:331
  83.1 9.4 %back.1 = f32[8,1024,512]{2,1,0:T(8,128)} custom-call(f32[32,2,512]{2,1,0:T(2,128)S(1)} %all_to_all.5.st_ref, f32[128,512]{1,0:T(8,128)S(1)} %get-tuple-element.11.pt_ref, bf16[64,512,128]{2,1,0:T(8,128)(2,1)S(1)} %get-tuple-element.12.y_ref, bf16[8,1024,512]{2,1,0:T(8,128)(2,1)S(1)} %get-tuple-element.13.x_ref, bf16[512,512]{1,0:T(8,128)(2,1)S(1)} %get-tuple-element.14.wo_ref), custom_call_target="tpu_custom_call" | custom-call | tf_op jit(solution)/shard_map/back/pallas_call | solution.py:335
  (17 shorter events, 0.2 us)
Async XLA Ops:
  1.7 7.6 %collective-permute-start.2 = (bf16[1,16,1664]{2,1,0:T(8,128)(2,1)}, bf16[1,16,1664]{2,1,0:T(8,128)(2,1)S(1)}, u32[]{:S(2)}, u32[]{:S(2)}) collective-permute-start(bf16[1,16,1664]{2,1,0:T(8,128)(2,1)} %bitcast.5), channel_id=1, source_target_pairs={{0,3},{1,2},{2,1},{3,0},{4,7},{5,6},{6,5},{7,4},{8,11},{9,10},{10,... | collective-permute-start | bytes 159752 | tf_op jit(solution)/shard_map/ppermute | solution.py:43
  6.7 5.2 %collective-permute-start.1 = (bf16[1,16,1664]{2,1,0:T(8,128)(2,1)}, bf16[1,16,1664]{2,1,0:T(8,128)(2,1)S(1)}, u32[]{:S(2)}, u32[]{:S(2)}) collective-permute-start(bf16[1,16,1664]{2,1,0:T(8,128)(2,1)} %bitcast.6), channel_id=1, source_target_pairs={{0,2},{1,3},{2,0},{3,1},{4,6},{5,7},{6,4},{7,5},{8,10},{9,11},{10,... | collective-permute-start | bytes 159752 | tf_op jit(solution)/shard_map/ppermute | solution.py:43
  6.7 5.2 %collective-permute-start = (bf16[1,16,1664]{2,1,0:T(8,128)(2,1)}, bf16[1,16,1664]{2,1,0:T(8,128)(2,1)S(1)}, u32[]{:S(2)}, u32[]{:S(2)}) collective-permute-start(bf16[1,16,1664]{2,1,0:T(8,128)(2,1)} %bitcast.7), channel_id=1, source_target_pairs={{0,1},{1,0},{2,3},{3,2},{4,5},{5,4},{6,7},{7,6},{8,9},{9,8},{10,11... | collective-permute-start | bytes 159752 | tf_op jit(solution)/shard_map/ppermute | solution.py:43
  12.8 9.2 %collective-permute-start.5 = (bf16[4,16,1664]{2,1,0:T(8,128)(2,1)S(1)}, bf16[4,16,1664]{2,1,0:T(8,128)(2,1)S(1)}, u32[]{:S(2)}, u32[]{:S(2)}) collective-permute-start(bf16[4,16,1664]{2,1,0:T(8,128)(2,1)S(1)} %pad_maximum_fusion.refs_0_), channel_id=1, source_target_pairs={{0,24},{4,28},{8,16},{12,20},{16,8},{20,12},{24,0},{28,4},{1,25},{... | collective-permute-start | bytes 638984 | tf_op jit(solution)/shard_map/ppermute | solution.py:43
  15.3 9.2 %collective-permute-start.4 = (bf16[4,16,1664]{2,1,0:T(8,128)(2,1)S(1)}, bf16[4,16,1664]{2,1,0:T(8,128)(2,1)S(1)}, u32[]{:S(2)}, u32[]{:S(2)}) collective-permute-start(bf16[4,16,1664]{2,1,0:T(8,128)(2,1)S(1)} %pad_maximum_fusion.refs_0_), channel_id=1, source_target_pairs={{0,16},{4,20},{8,24},{12,28},{16,0},{20,4},{24,8},{28,12},{1,17},{... | collective-permute-start | bytes 638984 | tf_op jit(solution)/shard_map/ppermute | solution.py:43
  15.9 8.8 %collective-permute-start.3 = (bf16[4,16,1664]{2,1,0:T(8,128)(2,1)S(1)}, bf16[4,16,1664]{2,1,0:T(8,128)(2,1)S(1)}, u32[]{:S(2)}, u32[]{:S(2)}) collective-permute-start(bf16[4,16,1664]{2,1,0:T(8,128)(2,1)S(1)} %pad_maximum_fusion.refs_0_), channel_id=1, source_target_pairs={{0,8},{4,12},{8,0},{12,4},{16,24},{20,28},{24,16},{28,20},{1,9},{5... | collective-permute-start | bytes 638984 | tf_op jit(solution)/shard_map/ppermute | solution.py:43
  17.4 7.7 %collective-permute-start.11 = (bf16[8,16,512]{2,1,0:T(8,128)(2,1)S(1)}, bf16[8,16,512]{2,1,0:T(8,128)(2,1)S(1)}, u32[]{:S(2)}, u32[]{:S(2)}) collective-permute-start(bf16[8,16,512]{2,1,0:T(8,128)(2,1)S(1)} %get-tuple-element.15), channel_id=1, source_target_pairs={{4,0},{8,4},{12,8},{16,12},{20,16},{24,20},{28,24},{5,1},{9,5},{13... | collective-permute-start | bytes 393224 | tf_op jit(solution)/shard_map/ppermute | solution.py:290
  18.7 10.0 %collective-permute-start.6 = (bf16[4,16,1664]{2,1,0:T(8,128)(2,1)S(1)}, bf16[4,16,1664]{2,1,0:T(8,128)(2,1)S(1)}, u32[]{:S(2)}, u32[]{:S(2)}) collective-permute-start(bf16[4,16,1664]{2,1,0:T(8,128)(2,1)S(1)} %pad_maximum_fusion.refs_0_), channel_id=1, source_target_pairs={{0,4},{4,0},{8,12},{12,8},{16,20},{20,16},{24,28},{28,24},{1,5},{5... | collective-permute-start | bytes 638984 | tf_op jit(solution)/shard_map/ppermute | solution.py:43
  22.0 6.8 %copy-start = (bf16[4,16,1664]{2,1,0:T(8,128)(2,1)}, bf16[4,16,1664]{2,1,0:T(8,128)(2,1)S(1)}, u32[]{:S(2)}) copy-start(bf16[4,16,1664]{2,1,0:T(8,128)(2,1)S(1)} %collective-permute-done.5.refs_3_) | copy-start | bytes 638980
  22.0 6.7 %collective-permute-start.9 = (bf16[4,16,1664]{2,1,0:T(8,128)(2,1)S(1)}, bf16[4,16,1664]{2,1,0:T(8,128)(2,1)S(1)}, u32[]{:S(2)}, u32[]{:S(2)}) collective-permute-start(bf16[4,16,1664]{2,1,0:T(8,128)(2,1)S(1)} %collective-permute-done.5.refs_3_), channel_id=1, source_target_pairs={{0,4},{4,0},{8,12},{12,8},{16,20},{20,16},{24,28},{28,24},{1,5},{5... | collective-permute-start | bytes 638984 | tf_op jit(solution)/shard_map/ppermute | solution.py:43
  24.5 4.2 %collective-permute-start.8 = (bf16[4,16,1664]{2,1,0:T(8,128)(2,1)S(1)}, bf16[4,16,1664]{2,1,0:T(8,128)(2,1)S(1)}, u32[]{:S(2)}, u32[]{:S(2)}) collective-permute-start(bf16[4,16,1664]{2,1,0:T(8,128)(2,1)S(1)} %collective-permute-done.4.refs_2_), channel_id=1, source_target_pairs={{0,4},{4,0},{8,12},{12,8},{16,20},{20,16},{24,28},{28,24},{1,5},{5... | collective-permute-start | bytes 638984 | tf_op jit(solution)/shard_map/ppermute | solution.py:43
  24.6 4.1 %collective-permute-start.7 = (bf16[4,16,1664]{2,1,0:T(8,128)(2,1)S(1)}, bf16[4,16,1664]{2,1,0:T(8,128)(2,1)S(1)}, u32[]{:S(2)}, u32[]{:S(2)}) collective-permute-start(bf16[4,16,1664]{2,1,0:T(8,128)(2,1)S(1)} %collective-permute-done.3.refs_1_), channel_id=1, source_target_pairs={{0,4},{4,0},{8,12},{12,8},{16,20},{20,16},{24,28},{28,24},{1,5},{5... | collective-permute-start | bytes 638984 | tf_op jit(solution)/shard_map/ppermute | solution.py:43
  25.0 3.7 %collective-permute-start.10 = (bf16[8,16,512]{2,1,0:T(8,128)(2,1)S(1)}, bf16[8,16,512]{2,1,0:T(8,128)(2,1)S(1)}, u32[]{:S(2)}, u32[]{:S(2)}) collective-permute-start(bf16[8,16,512]{2,1,0:T(8,128)(2,1)S(1)} %get-tuple-element.16), channel_id=1, source_target_pairs={{0,4},{4,8},{8,12},{12,16},{16,20},{20,24},{24,28},{1,5},{5,9},{9,... | collective-permute-start | bytes 393224 | tf_op jit(solution)/shard_map/ppermute | solution.py:289
  28.7 0.7 copy-start.1
  28.7 0.7 copy-start.2
  28.7 0.8 copy-start.3
  29.5 0.7 copy-start.4
